TPU v7x, 32 devices: a whole 2x2x4 slice. The times are simulated.
32 devices in a mesh: clip: 8 (over z, y), frame: 4 (over x, core).
Axes of the slice: x: 2, y: 2, z: 4, core: 2. Of those that a mesh axis runs over, the one named last changes fastest.
Arguments:
- inputs: bfloat16 [16, 8, 196, 768], P('clip', 'frame'), may hold values from -6 to 6
- out_grad: bfloat16 [16, 8, 196, 768], P('clip', 'frame'), may hold values from -6 to 6
- adapter_index: int32 [16], P('clip'), may hold values from 0 to 7, as said below
- norm_gain: bfloat16 [3, 768], P(None, 'clip'), may hold values from 0.5 to 1.5
- norm_bias: bfloat16 [3, 768], P(None, 'clip'), may hold values from -4 to 4
- qkv_weight: bfloat16 [2, 768, 2304], P(None, 'clip'), may hold values from -0.21875 to 0.21875
- proj_weight: bfloat16 [3, 768, 768], P(None, 'clip'), may hold values from -0.3125 to 0.3125
- mlp_in: bfloat16 [768, 3072], P('clip'), may hold values from -0.21875 to 0.21875
- mlp_out: bfloat16 [3072, 768], P('clip'), may hold values from -0.109375 to 0.109375
- adapt_down: bfloat16 [6, 8, 768, 16], P(None, None, 'clip'), may hold values from -0.21875 to 0.21875
- adapt_down_wide: bfloat16 [8, 3072, 16], P(None, 'clip'), may hold values from -0.109375 to 0.109375
- adapt_up_qkv: bfloat16 [2, 8, 16, 2304], P(None, None, None, 'clip'), may hold values from -1.5 to 1.5
- adapt_up: bfloat16 [4, 8, 16, 768], P(None, None, None, 'clip'), may hold values from -1.5 to 1.5
- adapt_up_wide: bfloat16 [8, 16, 3072], P(None, None, 'clip'), may hold values from -1.5 to 1.5
Outputs:
- output: bfloat16 [16, 8, 196, 768], P('clip', 'frame')
- input_grad: bfloat16 [16, 8, 196, 768], P('clip', 'frame')
- grad_down: float32 [6, 8, 768, 16], P(None, None, 'clip')
- grad_down_wide: float32 [8, 3072, 16], P(None, 'clip')
- grad_up_qkv: float32 [2, 8, 16, 2304], P(None, None, None, 'clip')
- grad_up: float32 [4, 8, 16, 768], P(None, None, None, 'clip')
- grad_up_wide: float32 [8, 16, 3072], P(None, None, 'clip')
Inputs may be any that keep to these rules, and one draw needn't show every extreme that they name: `adapter_index`: every one of the 8 adapters is chosen by at least one clip.
All inputs are finite; a program needn't handle non-finite values.
Results may differ from a plain program's by a relative error of at most 0.025.
Values may be sent and summed in bfloat16 or wider, within the bound.
A program may use at most 256 MiB of HBM per device.

v0:
```python
import jax
import jax.numpy as jnp
from jax import lax
from jax.sharding import PartitionSpec as P

HEADS = 12
HD = 64


score_scale = 0.125
eps_norm = 1e-06


def layer_norm(values, gains, shifts):
    row_mean = jnp.mean(values, axis=-1, keepdims=True)
    centred = values - row_mean
    spread = jnp.mean(centred * centred, axis=-1, keepdims=True)
    return centred * lax.rsqrt(spread + eps_norm) * gains + shifts


def norm_back(values, gains, shifts, grad_rows):
    _, pull = jax.vjp(lambda inner_vals: layer_norm(inner_vals, gains, shifts), values)
    return pull(grad_rows)[0]


def exact_gelu(values):
    return jax.nn.gelu(values, approximate=False)


def unpack(gathered, onehot):
    gains = gathered[0].astype(jnp.float32)
    shifts = gathered[1].astype(jnp.float32)

    def choose(form, table):
        return jnp.einsum(form, onehot, table, preferred_element_type=jnp.float32).astype(
            jnp.bfloat16
        )

    pick_down = choose("ca,kair->kcir", gathered[6])
    pick_down_wide = choose("ca,air->cir", gathered[7])
    pick_qkv = choose("ca,karo->kcro", gathered[8])
    pick_up = choose("ca,karo->kcro", gathered[9])
    pick_up_wide = choose("ca,aro->cro", gathered[10])
    return (
        gains,
        shifts,
        gathered[2],
        gathered[3],
        gathered[4],
        gathered[5],
        pick_down,
        pick_down_wide,
        pick_qkv,
        pick_up,
        pick_up_wide,
    )


def adapted_fwd(hidden, weight, down_factor, up_factor):
    inner_rank = jnp.einsum(
        "cni,cir->cnr", hidden, down_factor, preferred_element_type=jnp.float32
    ).astype(jnp.bfloat16)
    result = jnp.einsum("cni,io->cno", hidden, weight, preferred_element_type=jnp.float32)
    result = result + jnp.einsum(
        "cnr,cro->cno", inner_rank, up_factor, preferred_element_type=jnp.float32
    )
    return (result, inner_rank)


def adapted_back(grad_out, hidden, inner_rank, weight, down_factor, up_factor):
    grad_rank = jnp.einsum(
        "cno,cro->cnr", grad_out, up_factor, preferred_element_type=jnp.float32
    ).astype(jnp.bfloat16)
    grad_hidden = jnp.einsum("cno,io->cni", grad_out, weight, preferred_element_type=jnp.float32)
    grad_hidden = grad_hidden + jnp.einsum(
        "cnr,cir->cni", grad_rank, down_factor, preferred_element_type=jnp.float32
    )
    grad_first = jnp.einsum("cni,cnr->cir", hidden, grad_rank, preferred_element_type=jnp.float32)
    grad_second = jnp.einsum(
        "cnr,cno->cro", inner_rank, grad_out, preferred_element_type=jnp.float32
    )
    return (grad_hidden, grad_first, grad_second)


def attend(packed):
    queries = packed[:, :, 0]
    key_rows = packed[:, :, 1]
    value_rows = packed[:, :, 2]
    scores = (
        jnp.einsum("bshd,bthd->bhst", queries, key_rows, preferred_element_type=jnp.float32)
        * score_scale
    )
    attn_probs = jax.nn.softmax(scores, axis=-1)
    result = jnp.einsum(
        "bhst,bthd->bshd",
        attn_probs.astype(jnp.bfloat16),
        value_rows,
        preferred_element_type=jnp.float32,
    )
    return (result, attn_probs)


def attend_back(grad_out, packed, attn_probs):
    queries = packed[:, :, 0]
    key_rows = packed[:, :, 1]
    value_rows = packed[:, :, 2]
    grad_probs = jnp.einsum(
        "bshd,bthd->bhst", grad_out, value_rows, preferred_element_type=jnp.float32
    )
    grad_values = jnp.einsum(
        "bhst,bshd->bthd",
        attn_probs.astype(jnp.bfloat16),
        grad_out,
        preferred_element_type=jnp.float32,
    )
    grad_scores = attn_probs * (
        grad_probs - jnp.sum(grad_probs * attn_probs, axis=-1, keepdims=True)
    )
    grad_scores = grad_scores.astype(jnp.bfloat16)
    grad_queries = (
        jnp.einsum("bhst,bthd->bshd", grad_scores, key_rows, preferred_element_type=jnp.float32)
        * score_scale
    )
    grad_keys = (
        jnp.einsum("bhst,bshd->bthd", grad_scores, queries, preferred_element_type=jnp.float32)
        * score_scale
    )
    return jnp.stack([grad_queries, grad_keys, grad_values], axis=2).astype(jnp.bfloat16)


def per_device(
    inputs,
    out_grad,
    adapter_index,
    norm_gain,
    norm_bias,
    qkv_weight,
    proj_weight,
    mlp_in,
    mlp_out,
    adapt_down,
    adapt_down_wide,
    adapt_up_qkv,
    adapt_up,
    adapt_up_wide,
):
    clip_count, frame_part, patch_total, width = inputs.shape
    groups = lax.axis_size("frame")
    frame_total = frame_part * groups
    patch_part = patch_total // groups
    adapters = adapt_down_wide.shape[0]
    onehot = (adapter_index[:, None] == jnp.arange(adapters, dtype=jnp.int32)[None, :]).astype(
        jnp.bfloat16
    )
    gathered = (
        lax.all_gather(norm_gain, "clip", axis=1, tiled=True),
        lax.all_gather(norm_bias, "clip", axis=1, tiled=True),
        lax.all_gather(qkv_weight, "clip", axis=1, tiled=True),
        lax.all_gather(proj_weight, "clip", axis=1, tiled=True),
        lax.all_gather(mlp_in, "clip", axis=0, tiled=True),
        lax.all_gather(mlp_out, "clip", axis=0, tiled=True),
        lax.all_gather(adapt_down, "clip", axis=2, tiled=True),
        lax.all_gather(adapt_down_wide, "clip", axis=1, tiled=True),
        lax.all_gather(adapt_up_qkv, "clip", axis=3, tiled=True),
        lax.all_gather(adapt_up, "clip", axis=3, tiled=True),
        lax.all_gather(adapt_up_wide, "clip", axis=2, tiled=True),
    )
    (
        gains,
        shifts,
        w_qkv,
        w_proj,
        w_in,
        w_out,
        pick_down,
        pick_down_wide,
        pick_qkv,
        pick_up,
        pick_up_wide,
    ) = unpack(gathered, onehot)
    patch_rows = lax.all_to_all(inputs, "frame", split_axis=2, concat_axis=1, tiled=True)
    patch_float = patch_rows.astype(jnp.float32)
    hidden_t = (
        layer_norm(patch_float, gains[0], shifts[0])
        .astype(jnp.bfloat16)
        .reshape(clip_count, frame_total * patch_part, width)
    )
    qkv_t, rank_tq = adapted_fwd(hidden_t, w_qkv[0], pick_down[0], pick_qkv[0])
    qkv_tq = qkv_t.astype(jnp.bfloat16).reshape(clip_count, frame_total, patch_part, 3, HEADS, HD)
    qkv_tq = qkv_tq.transpose(0, 2, 1, 3, 4, 5).reshape(
        clip_count * patch_part, frame_total, 3, HEADS, HD
    )
    att_t, probs_t = attend(qkv_tq)
    att_tq = att_t.astype(jnp.bfloat16).reshape(clip_count, patch_part, frame_total, width)
    att_tq = att_tq.transpose(0, 2, 1, 3).reshape(clip_count, frame_total * patch_part, width)
    mid_t, rank_to = adapted_fwd(att_tq, w_proj[0], pick_down[1], pick_up[0])
    mid_tq = mid_t.astype(jnp.bfloat16)
    branch_t, rank_tf = adapted_fwd(mid_tq, w_proj[1], pick_down[2], pick_up[1])
    branch_tq = branch_t.astype(jnp.bfloat16).reshape(clip_count, frame_total, patch_part, width)
    branch_home = lax.all_to_all(branch_tq, "frame", split_axis=1, concat_axis=2, tiled=True)
    stream_one = inputs.astype(jnp.float32) + branch_home.astype(jnp.float32)
    token_rows = frame_part * patch_total
    hidden_s = (
        layer_norm(stream_one, gains[1], shifts[1])
        .astype(jnp.bfloat16)
        .reshape(clip_count, token_rows, width)
    )
    qkv_s, rank_sq = adapted_fwd(hidden_s, w_qkv[1], pick_down[3], pick_qkv[1])
    qkv_sq = qkv_s.astype(jnp.bfloat16).reshape(clip_count * frame_part, patch_total, 3, HEADS, HD)
    att_s, probs_s = attend(qkv_sq)
    att_sq = att_s.astype(jnp.bfloat16).reshape(clip_count, token_rows, width)
    branch_s, rank_so = adapted_fwd(att_sq, w_proj[2], pick_down[4], pick_up[2])
    stream_two = stream_one + branch_s.reshape(stream_one.shape)
    hidden_m = (
        layer_norm(stream_two, gains[2], shifts[2])
        .astype(jnp.bfloat16)
        .reshape(clip_count, token_rows, width)
    )
    pre_act, rank_f1 = adapted_fwd(hidden_m, w_in, pick_down[5], pick_up_wide)
    activ_q = exact_gelu(pre_act).astype(jnp.bfloat16)
    branch_m, rank_f2 = adapted_fwd(activ_q, w_out, pick_down_wide, pick_up[3])
    output = (stream_two + branch_m.reshape(stream_two.shape)).astype(jnp.bfloat16)
    regathered = (
        lax.all_gather(norm_gain, "clip", axis=1, tiled=True),
        lax.all_gather(norm_bias, "clip", axis=1, tiled=True),
        lax.all_gather(qkv_weight, "clip", axis=1, tiled=True),
        lax.all_gather(proj_weight, "clip", axis=1, tiled=True),
        lax.all_gather(mlp_in, "clip", axis=0, tiled=True),
        lax.all_gather(mlp_out, "clip", axis=0, tiled=True),
        lax.all_gather(adapt_down, "clip", axis=2, tiled=True),
        lax.all_gather(adapt_down_wide, "clip", axis=1, tiled=True),
        lax.all_gather(adapt_up_qkv, "clip", axis=3, tiled=True),
        lax.all_gather(adapt_up, "clip", axis=3, tiled=True),
        lax.all_gather(adapt_up_wide, "clip", axis=2, tiled=True),
    )
    (
        gains,
        shifts,
        w_qkv,
        w_proj,
        w_in,
        w_out,
        pick_down,
        pick_down_wide,
        pick_qkv,
        pick_up,
        pick_up_wide,
    ) = unpack(regathered, onehot)
    grad_top = out_grad.astype(jnp.float32)
    grad_mq = grad_top.astype(jnp.bfloat16).reshape(clip_count, token_rows, width)
    grad_act, down_f2, up_f2 = adapted_back(
        grad_mq, activ_q, rank_f2, w_out, pick_down_wide, pick_up[3]
    )
    _, gelu_pull = jax.vjp(exact_gelu, pre_act)
    grad_pre = gelu_pull(grad_act.astype(jnp.bfloat16).astype(jnp.float32))[0].astype(jnp.bfloat16)
    grad_hm, down_f1, up_f1 = adapted_back(
        grad_pre, hidden_m, rank_f1, w_in, pick_down[5], pick_up_wide
    )
    grad_two = grad_top + norm_back(
        stream_two, gains[2], shifts[2], grad_hm.reshape(stream_two.shape)
    )
    grad_sq = grad_two.astype(jnp.bfloat16).reshape(clip_count, token_rows, width)
    grad_att_s, down_so, up_so = adapted_back(
        grad_sq, att_sq, rank_so, w_proj[2], pick_down[4], pick_up[2]
    )
    grad_att_sq = grad_att_s.astype(jnp.bfloat16).reshape(
        clip_count * frame_part, patch_total, HEADS, HD
    )
    grad_qkv_s = attend_back(grad_att_sq, qkv_sq, probs_s).reshape(
        clip_count, token_rows, 3 * width
    )
    grad_hs, down_sq, up_sq = adapted_back(
        grad_qkv_s, hidden_s, rank_sq, w_qkv[1], pick_down[3], pick_qkv[1]
    )
    grad_one = grad_two + norm_back(
        stream_one, gains[1], shifts[1], grad_hs.reshape(stream_one.shape)
    )
    grad_patch = lax.all_to_all(
        grad_one.astype(jnp.bfloat16), "frame", split_axis=2, concat_axis=1, tiled=True
    )
    grad_patch = grad_patch.reshape(clip_count, frame_total * patch_part, width)
    grad_mid, down_tf, up_tf = adapted_back(
        grad_patch, mid_tq, rank_tf, w_proj[1], pick_down[2], pick_up[1]
    )
    grad_att_t, down_to, up_to = adapted_back(
        grad_mid.astype(jnp.bfloat16), att_tq, rank_to, w_proj[0], pick_down[1], pick_up[0]
    )
    grad_att_tq = grad_att_t.astype(jnp.bfloat16).reshape(
        clip_count, frame_total, patch_part, HEADS, HD
    )
    grad_att_tq = grad_att_tq.transpose(0, 2, 1, 3, 4).reshape(
        clip_count * patch_part, frame_total, HEADS, HD
    )
    grad_qkv_t = attend_back(grad_att_tq, qkv_tq, probs_t).reshape(
        clip_count, patch_part, frame_total, 3 * width
    )
    grad_qkv_t = grad_qkv_t.transpose(0, 2, 1, 3).reshape(
        clip_count, frame_total * patch_part, 3 * width
    )
    grad_ht, down_tq, up_tq = adapted_back(
        grad_qkv_t, hidden_t, rank_tq, w_qkv[0], pick_down[0], pick_qkv[0]
    )
    grad_temporal = norm_back(patch_float, gains[0], shifts[0], grad_ht.reshape(patch_float.shape))
    grad_home = lax.all_to_all(
        grad_temporal.astype(jnp.bfloat16), "frame", split_axis=1, concat_axis=2, tiled=True
    )
    input_grad = (grad_one + grad_home.astype(jnp.float32)).astype(jnp.bfloat16)
    onehot_float = onehot.astype(jnp.float32)

    def spread(choice_rows, per_clip):
        return jnp.einsum("ca,c...->a...", choice_rows, per_clip)

    grad_down = jnp.stack(
        [
            spread(onehot_float, down_tq),
            spread(onehot_float, down_to),
            spread(onehot_float, down_tf),
            spread(onehot_float, down_sq),
            spread(onehot_float, down_so),
            spread(onehot_float, down_f1),
        ]
    )
    grad_down_wide = spread(onehot_float, down_f2)
    grad_up_qkv = jnp.stack([spread(onehot_float, up_tq), spread(onehot_float, up_sq)])
    grad_up = jnp.stack(
        [
            spread(onehot_float, up_to),
            spread(onehot_float, up_tf),
            spread(onehot_float, up_so),
            spread(onehot_float, up_f2),
        ]
    )
    grad_up_wide = spread(onehot_float, up_f1)
    owned = (
        lax.psum_scatter(grad_down, "clip", scatter_dimension=2, tiled=True),
        lax.psum_scatter(grad_down_wide, "clip", scatter_dimension=1, tiled=True),
        lax.psum_scatter(grad_up_qkv, "clip", scatter_dimension=3, tiled=True),
        lax.psum_scatter(grad_up, "clip", scatter_dimension=3, tiled=True),
        lax.psum_scatter(grad_up_wide, "clip", scatter_dimension=2, tiled=True),
    )
    summed = (
        lax.psum(owned[0].astype(jnp.bfloat16), "frame").astype(jnp.float32),
        lax.psum(owned[1].astype(jnp.bfloat16), "frame").astype(jnp.float32),
        lax.psum(owned[2].astype(jnp.bfloat16), "frame").astype(jnp.float32),
        lax.psum(owned[3].astype(jnp.bfloat16), "frame").astype(jnp.float32),
        lax.psum(owned[4].astype(jnp.bfloat16), "frame").astype(jnp.float32),
    )
    return (output, input_grad, summed[0], summed[1], summed[2], summed[3], summed[4])


def solution(mesh):
    return jax.shard_map(
        per_device,
        mesh=mesh,
        in_specs=(
            P("clip", "frame", None, None),
            P("clip", "frame", None, None),
            P("clip"),
            P(None, "clip"),
            P(None, "clip"),
            P(None, "clip", None),
            P(None, "clip", None),
            P("clip", None),
            P("clip", None),
            P(None, None, "clip", None),
            P(None, "clip", None),
            P(None, None, None, "clip"),
            P(None, None, None, "clip"),
            P(None, None, "clip"),
        ),
        out_specs=(
            P("clip", "frame", None, None),
            P("clip", "frame", None, None),
            P(None, None, "clip", None),
            P(None, "clip", None),
            P(None, None, None, "clip"),
            P(None, None, None, "clip"),
            P(None, None, "clip"),
        ),
        check_vma=False,
    )
```

profile of v0, /device:TPU:0, one launch (start us, length us, event | category | flops | bytes accessed | tf_op | source)
XLA Modules:
  0.0 1383.1 jit_solution(116229386866848011)
XLA Ops:
  16.0 4.3 all-to-all-start
  20.9 22.6 %all-gather = bf16[8,96,3]{1,2,0:T(4,128)(2,1)S(1)} all-gather(bf16[1,96,3]{1,2,0:T(4,128)(2,1)S(1)} %bitcast.398), channel_id=1, replica_groups=mesh['clip'=8,'frame'=4] {'clip'}, dimensions={0}, use_global_device_ids=true | all-gather | bytes 5184 | tf_op jit(solution)/shard_map/all_gather | solution.py:156
  44.2 16.7 %all-gather.1 = bf16[8,96,3]{1,2,0:T(4,128)(2,1)S(1)} all-gather(bf16[1,96,3]{1,2,0:T(4,128)(2,1)S(1)} %bitcast.399), channel_id=1, replica_groups=mesh['clip'=8,'frame'=4] {'clip'}, dimensions={0}, use_global_device_ids=true | all-gather | bytes 5184 | tf_op jit(solution)/shard_map/all_gather | solution.py:157
  62.0 166.8 %all_gather.49 = bf16[4,8,16,768]{2,1,0,3:T(8,128)(2,1)} all-gather(bf16[4,8,16,96]{2,1,0,3:T(8,128)(2,1)S(1)} %copy.812), channel_id=1, replica_groups=mesh['clip'=8,'frame'=4] {'clip'}, dimensions={3}, use_global_device_ids=true | all-gather | bytes 884736 | tf_op jit(solution)/shard_map/all_gather | solution.py:165
  228.8 8.1 copy.813
  238.2 34.5 %all_gather.51 = bf16[8,16,3072]{2,0,1:T(8,128)(2,1)S(1)} all-gather(bf16[8,16,384]{2,0,1:T(8,128)(2,1)S(1)} %copy.843), channel_id=1, replica_groups=mesh['clip'=8,'frame'=4] {'clip'}, dimensions={2}, use_global_device_ids=true | all-gather | bytes 884736 | tf_op jit(solution)/shard_map/all_gather | solution.py:166
  275.9 37.8 %all_gather.53 = bf16[8,3072,16]{1,0,2:T(8,128)(2,1)} all-gather(bf16[8,384,16]{1,0,2:T(8,128)(2,1)} %copy.845), channel_id=1, replica_groups=mesh['clip'=8,'frame'=4] {'clip'}, dimensions={1}, use_global_device_ids=true | all-gather | bytes 884736 | tf_op jit(solution)/shard_map/all_gather | solution.py:163
  328.4 12.2 copy.800
  342.0 68.3 %all-gather.13.cloned.1.call-done = bf16[2,8,16,2304]{2,1,0,3:T(8,128)(2,1)} async-done(((bf16[2,8,16,288]{2,1,0,3:T(8,128)(2,1)}), bf16[2,8,16,2304]{2,1,0,3:T(8,128)(2,1)}) %all-gather.13.cloned.1.call-update) | async-done | bytes 1179664 | tf_op jit(solution)/shard_map/all_gather | solution.py:164
  410.2 10.5 copy.803
  421.9 97.5 %all-gather.9.cloned.1.call-done = bf16[2,768,2304]{2,1,0:T(8,128)(2,1)} async-done(((bf16[2,96,2304]{2,1,0:T(8,128)(2,1)}), bf16[2,768,2304]{2,1,0:T(8,128)(2,1)}) %all-gather.9.cloned.1.call-update) | async-done | bytes 7077904 | tf_op jit(solution)/shard_map/all_gather | solution.py:158
  519.5 5.3 fusion.32
  527.7 11.9 reshape.247
  539.6 7.5 copy.805
  548.5 34.2 %fusion.202 = (f32[98,12,8]{2,1,0:T(8,128)S(1)}, f32[98,12,8,8]{2,3,1,0:T(8,128)S(1)}) fusion(f32[98,12,8,8]{2,3,1,0:T(8,128)S(1)} %fusion.58), kind=kOutput, calls=%fused_computation.335 | output fusion | flops 301063 | bytes 639744 | tf_op jit(solution)/shard_map/sub | solution.py:93
  605.2 60.2 %all-gather.19.cloned.1.call-done = bf16[3072,768]{1,0:T(8,128)(2,1)} async-done(((bf16[384,768]{1,0:T(8,128)(2,1)}), bf16[3072,768]{1,0:T(8,128)(2,1)}) %all-gather.19.cloned.1.call-update) | async-done | bytes 4718608 | tf_op jit(solution)/shard_map/all_gather | solution.py:161
  665.4 8.6 fusion.19
  686.6 5.4 fusion.34
  694.9 11.9 reshape.299
  706.8 7.0 fusion.200
  713.8 4.8 copy.957
  718.6 4.9 copy.958
  723.5 5.3 copy.956
  728.8 7.3 fusion.66
  736.1 9.8 fusion.203
  752.0 5.3 copy.950
  757.4 5.1 reshape.300
  787.7 10.4 fusion.25
  798.0 7.9 fusion.55
  805.9 23.2 %multiply_convert_fusion.1 = (bf16[2,392,3072]{2,1,0:T(8,128)(2,1)S(1)}, f32[2,392,3072]{2,1,0:T(8,128)}) fusion(f32[2,392,3072]{2,1,0:T(8,128)S(1)} %get-tuple-element.112, u8[392,3072]{1,0:T(8,128)(4,1)S(1)} %get-tuple-element.64, u8[392,3072]{1,0:T(8,128)(4,1)S(1)} %get-tuple-element.63), kind=kLoop, calls=%fused_computation.22 | loop fusion | flops 168591360 | bytes 26492928 | tf_op jit(solution)/shard_map/convert_element_type | solution.py:220
  831.4 6.3 fusion.21
  842.6 11.7 fusion.7
  856.6 6.3 fusion.23
  867.7 5.6 multiply_reduce_fusion.5
  873.7 10.9 fusion.196
  895.5 4.8 reshape.301
  900.3 5.1 copy.863
  905.4 10.2 multiply_reduce_fusion
  915.7 11.3 multiply_convert_fusion
  933.4 5.7 fusion.59
  942.7 13.5 copy.954
  956.2 12.8 reshape.302
  972.2 5.0 fusion.33
  983.8 4.9 multiply_reduce_fusion.4
  989.1 9.7 fusion.195
  1019.4 4.7 all-to-all-done.2
  1030.0 19.4 %copy.946 = f32[4,8,16,768]{1,2,0,3:T(8,128)} copy(f32[4,8,16,768]{3,1,2,0:T(8,128)S(1)} %pad_maximum_fusion.2) | data formatting | bytes 3145728
  1049.4 19.3 %reshape.297 = f32[768,512]{1,0:T(8,128)} reshape(f32[768,4,16,8]{3,2,1,0:T(8,128)} %bitcast.349) | data formatting | bytes 3145728
  1079.6 8.1 multiply_reduce_fusion.2
  1087.7 5.2 multiply_convert_fusion.4
  1100.8 4.3 pad_maximum_fusion
  1105.1 9.8 copy.889
  1114.9 12.6 convert_element_type.342
  1127.5 4.8 copy.890
  1134.7 19.4 %copy.944 = f32[2,8,16,2304]{1,2,0,3:T(8,128)} copy(f32[2,8,16,2304]{3,1,2,0:T(8,128)S(1)} %pad_maximum_fusion.1) | data formatting | bytes 4718592
  1154.2 28.3 %reshape.295 = f32[2304,256]{1,0:T(8,128)} reshape(f32[2304,2,16,8]{3,2,1,0:T(8,128)} %bitcast.347) | data formatting | bytes 4718592
  1189.9 28.4 %copy.942 = f32[6,8,768,16]{1,3,0,2:T(8,128)} copy(f32[6,8,768,16]{2,1,3,0:T(8,128)S(1)} %fusion.81) | data formatting | bytes 4718592
  1218.3 27.0 %reshape.293 = f32[768,768]{1,0:T(8,128)} reshape(f32[768,6,16,8]{3,2,1,0:T(8,128)} %bitcast.348) | data formatting | bytes 4718592
  1245.6 6.2 fusion.31
  1261.5 4.8 fusion.45
  1266.3 18.5 %all_to_all.42 = bf16[2,8,49,768]{3,0,2,1:T(2,128)(2,1)S(1)} all-to-all(bf16[2,8,49,768]{3,0,2,1:T(2,128)(2,1)S(1)} %fusion.45), channel_id=1, replica_groups=mesh['clip'=8,'frame'=4] {'frame'}, dimensions={1} | all-to-all | bytes 2408448 | tf_op jit(solution)/shard_map/all_to_all | solution.py:304
  1301.9 23.5 %reduce-scatter.16.cloned.1.call-done = f32[96,768]{1,0:T(8,128)} async-done(((f32[768,768]{1,0:T(8,128)}), f32[96,768]{1,0:T(8,128)}) %reduce-scatter.16.cloned.1.call-update) | async-done | bytes 294928
  1325.4 4.7 reshape.294
  1337.6 30.0 %all-reduce.3.cloned.1.call-done = (bf16[6,8,96,16]{2,1,3,0:T(8,128)(2,1)}, bf16[8,384,16]{1,0,2:T(8,128)(2,1)}, bf16[2,8,16,288]{3,1,2,0:T(8,128)(2,1)}, bf16[4...) async-done(((bf16[6,8,96,16]{2,1,3,0:T(8,128)(2,1)}, bf16[8,384,16]{1,0,2:T(8,128)(2,1)}, bf16[2,8,16,288]{3,1,2,0:T(8,128)(2,1)}, bf16[4,8,16,96]{3,1,2,0:T(8,128)(2,1)}, ...) | async-done | bytes 589840 | tf_op jit(solution)/shard_map/psum | solution.py:342
  (465 shorter events, 248.4 us)
Async XLA Ops:
  7.2 321.2 %all-gather.11.cloned.1.call-start = ((), (), s32[]{:S(2)}) async-start(), calls=%async_computation.10 | async-start | bytes 10616832 | tf_op jit(solution)/shard_map/all_gather | solution.py:162
  10.0 400.2 %all-gather.13.cloned.1.call-start = ((), (), s32[]{:S(2)}) async-start(), calls=%async_computation.11 | async-start | bytes 10616832 | tf_op jit(solution)/shard_map/all_gather | solution.py:164
  12.2 507.3 %all-gather.9.cloned.1.call-start = ((), (), s32[]{:S(2)}) async-start(), calls=%async_computation.9 | async-start | bytes 7962624 | tf_op jit(solution)/shard_map/all_gather | solution.py:158
  12.9 578.8 %all-gather.15.cloned.1.call-start = ((), (), s32[]{:S(2)}) async-start(), calls=%async_computation.12 | async-start | bytes 3981312 | tf_op jit(solution)/shard_map/all_gather | solution.py:159
  13.5 651.9 %all-gather.19.cloned.1.call-start = ((), (), s32[]{:S(2)}) async-start(), calls=%async_computation.14 | async-start | bytes 5308416 | tf_op jit(solution)/shard_map/all_gather | solution.py:161
  14.1 6.8 copy-start.118
  14.1 30.0 %copy-start.119 = (bf16[3,96]{1,0:T(4,128)(2,1)S(1)}, bf16[3,96]{1,0:T(4,128)(2,1)}, u32[]{:S(2)}) copy-start(bf16[3,96]{1,0:T(4,128)(2,1)} %param.18) | copy-start | bytes 1732
  14.1 46.8 %copy-start.98 = (bf16[4,8,16,96]{3,2,1,0:T(8,128)(2,1)S(1)}, bf16[4,8,16,96]{3,2,1,0:T(8,128)(2,1)}, u32[]{:S(2)}) copy-start(bf16[4,8,16,96]{3,2,1,0:T(8,128)(2,1)} %param.26) | copy-start | bytes 294916
  16.0 297.7 %all-to-all-start = ((bf16[2,2,196,768]{3,1,0,2:T(2,128)(2,1)}), bf16[2,2,196,768]{3,1,0,2:T(2,128)(2,1)}, u32[]{:S(2)}, u32[]{:S(2)}) async-start(bf16[2,2,196,768]{3,1,0,2:T(2,128)(2,1)} %copy.785), calls=%async_computation | async-start | bytes 2408448 | tf_op jit(solution)/shard_map/all_to_all | solution.py:181
  20.3 767.4 %all-gather.17.cloned.1.call-start = ((), (), s32[]{:S(2)}) async-start(), calls=%async_computation.13 | async-start | bytes 5308416 | tf_op jit(solution)/shard_map/all_gather | solution.py:160
  44.2 283.8 %copy-start.92 = (f32[768]{0:T(1024)}, f32[768]{0:T(1024)S(1)}, u32[]{:S(2)}) copy-start(f32[768]{0:T(1024)S(1)} %get-tuple-element.67) | copy-start | bytes 9220
  228.8 8.1 copy-start.89
  228.8 9.4 copy-start.99
  237.0 36.4 %copy-start.100 = (bf16[8,384,16]{1,2,0:T(8,128)(2,1)S(1)}, bf16[8,384,16]{1,2,0:T(8,128)(2,1)}, u32[]{:S(2)}) copy-start(bf16[8,384,16]{1,2,0:T(8,128)(2,1)} %param.24) | copy-start | bytes 294916
  237.0 37.0 %copy-start.22 = (bf16[2,2,196,768]{3,1,2,0:T(2,128)(2,1)S(1)}, bf16[2,2,196,768]{3,1,2,0:T(2,128)(2,1)}, u32[]{:S(2)}) copy-start(bf16[2,2,196,768]{3,1,2,0:T(2,128)(2,1)} %param.15) | copy-start | bytes 3612676
  238.2 36.7 %copy-start.68 = (bf16[2,16,768]{2,0,1:T(2,128)(2,1)}, bf16[2,16,768]{2,0,1:T(2,128)(2,1)S(1)}, u32[]{:S(2)}) copy-start(bf16[2,16,768]{2,0,1:T(2,128)(2,1)S(1)} %get-tuple-element.100) | copy-start | bytes 147460
  274.4 39.3 %copy-start.25 = (bf16[2,392,768]{2,1,0:T(8,128)(2,1)}, bf16[2,392,768]{2,1,0:T(8,128)(2,1)S(1)}, u32[]{:S(2)}) copy-start(bf16[2,392,768]{2,1,0:T(8,128)(2,1)S(1)} %reshape.258) | copy-start | bytes 3612676
  315.8 8.0 copy-start
  316.6 7.2 copy-start.33
  318.4 5.2 copy-start.103
  318.7 9.2 copy-start.114
  318.8 9.1 copy-start.112
  328.4 93.1 %copy-start.18 = (bf16[2,392,768]{2,1,0:T(8,128)(2,1)}, bf16[2,392,768]{2,1,0:T(8,128)(2,1)S(1)}, u32[]{:S(2)}) copy-start(bf16[2,392,768]{2,1,0:T(8,128)(2,1)S(1)} %add_convert_fusion.11) | copy-start | bytes 3612676
  342.0 79.5 %copy-start.59 = (bf16[2,768,16]{1,0,2:T(2,128)(2,1)}, bf16[2,768,16]{1,0,2:T(2,128)(2,1)S(1)}, u32[]{:S(2)}) copy-start(bf16[2,768,16]{1,0,2:T(2,128)(2,1)S(1)} %get-tuple-element.97) | copy-start | bytes 147460
  421.5 103.3 %copy-start.57 = (bf16[2,16,2304]{2,0,1:T(2,128)(2,1)}, bf16[2,16,2304]{2,0,1:T(2,128)(2,1)S(1)}, u32[]{:S(2)}) copy-start(bf16[2,16,2304]{2,0,1:T(2,128)(2,1)S(1)} %get-tuple-element.99) | copy-start | bytes 442372
  421.5 270.5 %copy-start.49 = (bf16[2,16,2304]{2,0,1:T(2,128)(2,1)}, bf16[2,16,2304]{2,0,1:T(2,128)(2,1)S(1)}, u32[]{:S(2)}) copy-start(bf16[2,16,2304]{2,0,1:T(2,128)(2,1)S(1)} %get-tuple-element.98) | copy-start | bytes 442372
  421.9 102.9 %copy-start.78 = (bf16[2,392,16]{1,2,0:T(8,128)(2,1)}, bf16[2,392,16]{1,2,0:T(8,128)(2,1)S(1)}, u32[]{:S(2)}) copy-start(bf16[2,392,16]{1,2,0:T(8,128)(2,1)S(1)} %convolution_convert_fusion.17) | copy-start | bytes 75268
  547.1 35.7 %copy-start.5 = (bf16[2,49,8,3,12,64]{5,2,4,1,0,3:T(8,128)(2,1)}, bf16[2,49,8,3,12,64]{5,2,4,1,0,3:T(8,128)(2,1)S(1)}, u32[]{:S(2)}) copy-start(bf16[2,49,8,3,12,64]{5,2,4,1,0,3:T(8,128)(2,1)S(1)} %copy.805) | copy-start | bytes 10838020
  598.5 5.6 copy-start.41
  598.5 5.6 copy-start.90
  598.5 66.9 %copy-start.26 = (bf16[2,392,768]{2,1,0:T(8,128)(2,1)S(1)}, bf16[2,392,768]{2,1,0:T(8,128)(2,1)}, u32[]{:S(2)}) copy-start(bf16[2,392,768]{2,1,0:T(8,128)(2,1)} %copy-done.25) | copy-start | bytes 3612676
  600.5 73.5 %all-to-all-start.1 = ((bf16[2,8,49,768]{3,0,2,1:T(2,128)(2,1)}), bf16[2,8,49,768]{3,0,2,1:T(2,128)(2,1)S(1)}, u32[]{:S(2)}, u32[]{:S(2)}) async-start(bf16[2,8,49,768]{3,0,2,1:T(2,128)(2,1)} %bitcast.380), calls=%async_computation.1 | async-start | bytes 2408448 | tf_op jit(solution)/shard_map/all_to_all | solution.py:200
  604.0 683.1 %reduce-scatter.14.cloned.1.call-start = ((), (), s32[]{:S(2)}) async-start(), calls=%async_computation.16 | async-start | bytes 1769472 | tf_op jit(solution)/shard_map/reduce_scatter | solution.py:339
  686.6 5.4 copy-start.80
  736.1 13.6 copy-start.47
  745.9 6.2 copy-start.82
  805.9 23.3 %copy-start.32 = (f32[2,392,3072]{2,1,0:T(8,128)}, f32[2,392,3072]{2,1,0:T(8,128)S(1)}, u32[]{:S(2)}) copy-start(f32[2,392,3072]{2,1,0:T(8,128)S(1)} %get-tuple-element.112) | copy-start | bytes 28901380
  805.9 23.3 %copy-start.56 = (bf16[2,3072,16]{1,0,2:T(2,128)(2,1)S(1)}, bf16[2,3072,16]{1,0,2:T(2,128)(2,1)}, u32[]{:S(2)}) copy-start(bf16[2,3072,16]{1,0,2:T(2,128)(2,1)} %convolution_convert_fusion.1) | copy-start | bytes 589828
  831.4 6.3 copy-start.69
  856.6 6.4 copy-start.72
  873.6 10.9 copy-start.23
  931.7 7.3 slice-start
  933.4 5.7 slice-start.1
  956.2 12.8 copy-start.50
  983.8 5.2 copy-start.45
  989.1 9.7 copy-start.11
  989.1 9.7 copy-start.24
  1002.4 5.6 copy-start.30
  1004.3 19.8 %all-to-all-start.2 = ((bf16[2,2,196,768]{3,1,0,2:T(2,128)(2,1)}), bf16[2,2,196,768]{3,1,0,2:T(2,128)(2,1)S(1)}, u32[]{:S(2)}, u32[]{:S(2)}) async-start(bf16[2,2,196,768]{3,1,0,2:T(2,128)(2,1)} %copy.878), calls=%async_computation.2 | async-start | bytes 2408448 | tf_op jit(solution)/shard_map/all_to_all | solution.py:278
  1007.9 280.8 %reduce-scatter.12.cloned.1.call-start = ((), (), s32[]{:S(2)}) async-start(), calls=%async_computation.15 | async-start | bytes 1769472 | tf_op jit(solution)/shard_map/reduce_scatter | solution.py:336
  1013.1 277.2 %reduce-scatter.20.cloned.1.call-start = ((), (), s32[]{:S(2)}) async-start(), calls=%async_computation.19 | async-start | bytes 1769472
  1017.9 7.1 copy-start.75
  1017.9 7.4 copy-start.85
  1049.4 19.3 %copy-start.62 = (bf16[2,16,768]{2,0,1:T(2,128)(2,1)S(1)}, bf16[2,16,768]{2,0,1:T(2,128)(2,1)}, u32[]{:S(2)}) copy-start(bf16[2,16,768]{2,0,1:T(2,128)(2,1)} %get-tuple-element.103) | copy-start | bytes 147460
  1079.6 8.1 copy-start.55
  1087.7 207.7 %reduce-scatter.18.cloned.1.call-start = ((), (), s32[]{:S(2)}) async-start(), calls=%async_computation.18 | async-start | bytes 2654208
  1087.7 11.6 slice-start.2
  1092.9 6.5 slice-start.3
  1154.2 28.4 %copy-start.73 = (bf16[2,392,16]{1,2,0:T(8,128)(2,1)S(1)}, bf16[2,392,16]{1,2,0:T(8,128)(2,1)}, u32[]{:S(2)}) copy-start(bf16[2,392,16]{1,2,0:T(8,128)(2,1)} %copy-done.72) | copy-start | bytes 75268
  1182.5 142.9 %reduce-scatter.16.cloned.1.call-start = ((), (), s32[]{:S(2)}) async-start(), calls=%async_computation.17 | async-start | bytes 2654208
  1218.3 27.1 %copy-start.104 = (f32[2,4,2,49]{3,2,1,0:T(2,128)S(1)}, f32[2,4,2,49]{3,2,1,0:T(2,128)}, u32[]{:S(2)}) copy-start(f32[2,4,2,49]{3,2,1,0:T(2,128)} %copy-done.103) | copy-start | bytes 9412
  1245.4 122.3 %all-reduce.3.cloned.1.call-start = ((), (), s32[]{:S(2)}) async-start(), calls=%async_computation.20 | async-start | bytes 1441792 | tf_op jit(solution)/shard_map/psum | solution.py:342
  1245.6 6.2 copy-start.60
  1301.9 31.8 %copy-start.31 = (f32[2,2,196,768]{3,1,2,0:T(2,128)S(1)}, f32[2,2,196,768]{3,1,2,0:T(2,128)}, u32[]{:S(2)}) copy-start(f32[2,2,196,768]{3,1,2,0:T(2,128)} %get-tuple-element.77) | copy-start | bytes 7225348
  (75 other events, 210.9 us)
Sparse Core Ops, SparseCore 0:
  10.8 247.8 all-gather.10
  260.8 149.3 all-gather.12
  412.4 106.9 all-gather.8
  521.5 63.3 all-gather.14
  586.9 78.3 all-gather.18
  667.4 78.0 all-gather.16
  983.9 62.7 reduce-scatter.13
  1050.6 63.6 reduce-scatter.11
  1117.7 63.7 reduce-scatter.19
  1185.3 67.8 reduce-scatter.17
  1257.1 68.1 reduce-scatter.15
  1333.8 33.7 all-reduce.2
where the time goes:
time: 1390 us; the launch traced here: 1380 us
  local copies, waits for them, and re-layouts  407 us (29%)
  blocking collectives  297 us (21%)
  waiting for transfers between devices  287 us (21%)
  matrix products  198 us (14%)
  other arithmetic  166 us (12%)
  between operations  16.5 us (1%)
    unnamed x275, local copies, waits for them, and re-layouts  209 us
    all_gather x1, blocking collectives, per_device(): lax.all_gather(adapt_up, 'clip', axis=3, tiled=True)  167 us
    all_gather x1, waiting for transfers between devices, per_device(): lax.all_gather(qkv_weight, 'clip', axis=1, tiled=True)  97.5 us
    all_gather x1, waiting for transfers between devices, per_device(): lax.all_gather(adapt_up_qkv, 'clip', axis=3, tiled=True)  68.3 us
    all_gather x1, waiting for transfers between devices, per_device(): lax.all_gather(mlp_out, 'clip', axis=0, tiled=True)  60.2 us
    sub x2, other arithmetic, attend(): attn_probs = jax.nn.softmax(scores, axis=-1)  44 us
    convert_element_type x3, local copies, waits for them, and re-layouts, attend_back(): jnp.stack([grad_queries, grad_keys, grad_values], axis=2)  38.9 us
    all_gather x1, blocking collectives, per_device(): lax.all_gather(adapt_down_wide, 'clip', axis=1, tiled=True)  37.8 us
  transfers between devices with their start and end apart: 15, of which 6 were waited for; matrix products, arithmetic and copies ran while one was open for 39% of the time, Pallas kernels for 0%

commit v1 on v0

v1 whole, which is shorter than its diff:
```python
import functools
import jax
import jax.numpy as jnp
from jax import lax
from jax.experimental import pallas as pl
from jax.experimental.pallas import tpu as pltpu
from jax.sharding import PartitionSpec as P

EPS = 1e-06
MESH = pl.DeviceIdType.MESH
f32 = jnp.float32
bf16 = jnp.bfloat16
D, FF, QKV, RANK = 768, 3072, 2304, 16
NP, GR, R = 196, 208, 832
DOWN = (0, 768, 1536, 2304, 3072, 3840, 4608)
UP = (7680, 12288, 13056, 9984, 13824, 15360, 14592)
ADW = 18432
BIG = 1e30


def dg(a, b, ca, cb):
    return lax.dot_general(a, b, (((ca,), (cb,)), ((), ())), preferred_element_type=f32)


def iota(shape, d):
    return lax.broadcasted_iota(jnp.int32, shape, d)


def cols(off, w):
    return pl.ds(off if isinstance(off, int) else pl.multiple_of(off, 128), w)


def normal_parts(v):
    e = jnp.exp(-0.5 * v * v)
    t = 1.0 / (1.0 + 0.2316419 * jnp.abs(v))
    poly = t * (
        0.127414796
        + t * (-0.142248368 + t * (0.7107068705 + t * (-0.7265760135 + t * 0.5307027145)))
    )
    tail = poly * e
    return jnp.where(v >= 0, 1.0 - tail, tail), e


def onehot(col, width):
    return jnp.where(iota((col.shape[0], width), 1) == col, 1.0, 0.0).astype(bf16)


def message_rows():
    m = iota((GR, 1), 0)
    c = jnp.where(m >= 98, 1, 0)
    rest = m - 98 * c
    f = jnp.where(rest >= 49, 1, 0)
    return m < 196, c, f, rest - 49 * f


def to_message(owner):
    ok, c, f, q = message_rows()
    return jnp.where(ok, (2 * c + f) * GR + 49 * owner + q, -1)


def from_patches(owner):
    ok, c, f, q = message_rows()
    return jnp.where(ok, 392 * c + 8 * q + 2 * owner + f, -1)


def to_patches(chunk):
    t = iota((GR, 1), 0) + chunk * GR
    c = jnp.where(t >= 392, 1, 0)
    u = t - 392 * c
    q, fr = u >> 3, u & 7
    return jnp.where(t < 784, (fr >> 1) * GR + c * 98 + (fr & 1) * 49 + q, -1)


def to_frames(g):
    p = iota((GR, 1), 0)
    d = jnp.where(p >= 49, 1, 0) + jnp.where(p >= 98, 1, 0) + jnp.where(p >= 147, 1, 0)
    return jnp.where(p < NP, d * GR + (g // 2) * 98 + (g % 2) * 49 + p - 49 * d, -1)


def clip_mask(first):
    return (iota((R, 32), 0) >= first) == (iota((R, 32), 1) >= 16)


class Part:
    def __init__(self, ref, c0=0, width=None):
        self.ref, self.c0 = ref, c0
        self.width = ref.shape[1] - c0 if width is None else width

    def get(self, rows=slice(None), off=0, width=None):
        return self.ref[rows, cols(self.c0 + off, self.width if width is None else width)]

    def put(self, val, rows=slice(None), off=0):
        self.ref[rows, cols(self.c0 + off, val.shape[1])] = val


def chunks(size, body):
    @pl.loop(0, R // size)
    def _(i):
        body(pl.ds(pl.multiple_of(i * size, size), size))


def tiles(total, tile, body):
    if total == tile:
        body(0)
    else:

        @pl.loop(0, total // tile)
        def _(i):
            body(i * tile)


def norm_rows(v):
    mean = jnp.mean(v, axis=-1, keepdims=True)
    cen = v - mean
    rstd = lax.rsqrt(jnp.mean(cen * cen, axis=-1, keepdims=True) + EPS)
    return cen * rstd, rstd


def norm_back_rows(v, gain, dh):
    hat, rstd = norm_rows(v)
    g = dh * gain
    m1 = jnp.mean(g, axis=-1, keepdims=True)
    m2 = jnp.mean(g * hat, axis=-1, keepdims=True)
    return rstd * (g - m1 - hat * m2)


def head_masks(n):
    first = iota((n, 128), 1) < 64
    one, zero = jnp.ones((n, 128), bf16), jnp.zeros((n, 128), bf16)
    return jnp.where(first, one, zero), jnp.where(first, zero, one)


def attend_pair(qkv, rows, n, off, bias, out):
    q = qkv.get(rows, off, 128)
    k = qkv.get(rows, D + off, 128)
    v = qkv.get(rows, 2 * D + off, 128)
    o = None
    for hm in head_masks(n):
        s = dg(q, k * (hm * 0.125).astype(bf16), 1, 1) + bias
        p = jnp.exp(s - jnp.max(s, axis=-1, keepdims=True))
        p = p * (1.0 / jnp.sum(p, axis=-1, keepdims=True))
        oh = dg(p.astype(bf16), v * hm, 1, 0)
        o = oh if o is None else o + oh
    out.put(o.astype(bf16), rows, off)


def attend_pair_back(qkv, rows, n, off, bias, dout):
    q = qkv.get(rows, off, 128)
    k = qkv.get(rows, D + off, 128)
    v = qkv.get(rows, 2 * D + off, 128)
    do = dout.get(rows, off, 128)
    dq, dks, dvs = None, [], []
    for hm in head_masks(n):
        kh = k * (hm * 0.125).astype(bf16)
        s = dg(q, kh, 1, 1) + bias
        p = jnp.exp(s - jnp.max(s, axis=-1, keepdims=True))
        p = p * (1.0 / jnp.sum(p, axis=-1, keepdims=True))
        dp = dg(do, v * hm, 1, 1)
        dvs.append(dg(p.astype(bf16), do, 0, 0))
        ds = (p * (dp - jnp.sum(dp * p, axis=-1, keepdims=True))).astype(bf16)
        dqh = dg(ds, kh, 1, 0)
        dq = dqh if dq is None else dq + dqh
        dks.append(dg(ds, q, 0, 0))
    first = iota((n, 128), 1) < 64
    qkv.put(dq.astype(bf16), rows, off)
    qkv.put((jnp.where(first, dks[0], dks[1]) * 0.125).astype(bf16), rows, D + off)
    qkv.put(jnp.where(first, dvs[0], dvs[1]).astype(bf16), rows, 2 * D + off)


def spatial_loop(body):
    bias = jnp.where(iota((1, GR), 1) < NP, 0.0, -BIG)

    @pl.loop(0, 24)
    def _(i):
        rows = pl.ds(pl.multiple_of((i // 6) * GR, 16), GR)
        body(rows, GR, (i % 6) * 128, bias)


def temporal_loop(body):
    def bias(n):
        return jnp.where((iota((n, n), 0) >> 3) == (iota((n, n), 1) >> 3), 0.0, -BIG)

    @pl.loop(0, 6)
    def _(i):
        for h in range(6):
            body(pl.ds(pl.multiple_of(i * 128, 128), 128), 128, h * 128, bias(128))

    for h in range(6):
        body(pl.ds(768, 64), 64, h * 128, bias(64))


def layer_kernel(
    x_ref, g_ref, ad, nm, hq, hp, hi, ho,
    out, ig, gd, spill,
    wq, wp, wi, wo, snd, rcv_a, rcv_b, buf_g, buf_d, x1, x2, tmp, o2, qkv2, a0, a1, us,
    wsem, ssem, rsem, psem,
):
    clip = lax.axis_index("clip")
    me = lax.axis_index("frame")
    nf = 4
    peers = [lax.rem(me + k, nf) for k in range(1, nf)]

    loads = {}
    for key, src, dst in (
        ("q0", hq.at[0], wq.at[0]), ("p0", hp.at[0], wp.at[0]), ("p1", hp.at[1], wp.at[1]),
        ("q1", hq.at[1], wq.at[1]), ("p2", hp.at[2], wp.at[2]), ("o", ho, wo), ("i", hi, wi),
    ):
        loads[key] = pltpu.make_async_copy(src, dst, wsem.at[len(loads)])
        loads[key].start()

    barrier = pltpu.get_barrier_semaphore()
    for d in peers:
        pl.semaphore_signal(barrier, inc=1, device_id={"clip": clip, "frame": d}, device_id_type=MESH)
    pl.semaphore_wait(barrier, nf - 1)

    def exchange(step, src, index, rcv):
        sent = []
        for k, d in enumerate(peers):
            slot = pl.ds(k * GR, GR)
            snd[slot, :] = dg(onehot(index(d), R), src.get(), 1, 0).astype(bf16)
            cp = pltpu.make_async_remote_copy(
                src_ref=snd.at[slot],
                dst_ref=rcv.at[pl.ds(pl.multiple_of(me * GR, 16), GR)],
                send_sem=ssem.at[step, k],
                recv_sem=rsem.at[step, k],
                device_id={"clip": clip, "frame": d},
                device_id_type=MESH,
            )
            cp.start()
            sent.append(cp)
        rcv[pl.ds(pl.multiple_of(me * GR, 16), GR), :] = dg(onehot(index(me), R), src.get(), 1, 0).astype(bf16)

        def finish():
            for cp in sent:
                cp.wait_recv()
            for cp in sent:
                cp.wait_send()

        return finish

    def gain(k):
        return nm[k : k + 1, :]

    def norm(k, read, put):
        def body(rows):
            hat, _ = norm_rows(read(rows))
            put(rows, (hat * gain(k) + gain(3 + k)).astype(bf16))

        chunks(64, body)

    def rank(h, at, mask, m):
        us[m] = jnp.where(mask, dg(h.get(), ad[:, pl.ds(at, h.width)], 1, 1), 0.0).astype(bf16)

    def forward(m, h, w, width, tile, mask, emit):
        rank(h, DOWN[m], mask, m)

        def body(c):
            acc = dg(h.get(), w[:, cols(c, tile)], 1, 0)
            acc = acc + dg(us[m], ad[:, cols(UP[m] + c, tile)], 1, 0)
            emit(c, acc)

        tiles(width, tile, body)

    def backward(m, dz, w, width, tile, mask, emit):
        du = jnp.where(mask, dg(dz.get(), ad[:, pl.ds(UP[m], dz.width)], 1, 1), 0.0).astype(bf16)
        us[7] = du

        def body(c):
            acc = dg(dz.get(), w[cols(c, tile), :], 1, 1)
            acc = acc + dg(us[7], ad[:, cols(DOWN[m] + c, tile)], 1, 0)
            emit(c, acc)

        tiles(width, tile, body)

    def adapter_grads(m, h, dz):
        gd[:, pl.ds(DOWN[m], h.width)] = dg(us[7], h.get(), 0, 0).astype(gd.dtype)
        gd[:, pl.ds(UP[m], dz.width)] = dg(us[m], dz.get(), 0, 0).astype(gd.dtype)

    p_a0, p_a1 = Part(a0), Part(a1)
    qkv1, h1 = Part(buf_g, 0, QKV), Part(buf_g, QKV, D)
    xt, o1, m1, spare = (Part(buf_d, D * i, D) for i in range(4))
    p_o2, p_qkv2, p_g, p_d = Part(o2), Part(qkv2), Part(buf_g), Part(buf_d)

    for src, dst in ((x_ref, a0), (g_ref, a1)):
        for g in range(4):
            dst[pl.ds(GR * g + 192, 16), :] = jnp.zeros((16, D), bf16)
            dst[pl.ds(GR * g, NP), :] = src[g // 2, g % 2]
        if dst is a0:
            arrive = exchange(0, p_a0, to_message, rcv_a)

    mask_t = clip_mask(392)
    mask_s = clip_mask(416)
    arrive()
    for i in range(4):
        xt.put(dg(onehot(to_patches(i), R), rcv_a[...], 1, 0).astype(bf16), pl.ds(i * GR, GR))
    norm(0, lambda rows: xt.get(rows).astype(f32), lambda rows, v: h1.put(v, rows))
    loads["q0"].wait()
    forward(0, h1, wq.at[0], QKV, 768, mask_t, lambda c, acc: qkv1.put(acc.astype(bf16), off=c))
    temporal_loop(lambda rows, n, off, bias: attend_pair(qkv1, rows, n, off, bias, o1))
    loads["p0"].wait()
    forward(1, o1, wp.at[0], D, 384, mask_t, lambda c, acc: m1.put(acc.astype(bf16), off=c))
    loads["p1"].wait()
    forward(2, m1, wp.at[1], D, 384, mask_t, lambda c, acc: spare.put(acc.astype(bf16), off=c))
    arrive = exchange(1, spare, from_patches, rcv_b)
    saves = [pltpu.make_async_copy(b, spill.at[i], psem.at[i]) for i, b in enumerate((buf_g, buf_d))]
    for cp in saves:
        cp.start()
    for cp in saves:
        cp.wait()

    loads["o"].wait()
    backward(6, p_a1, wo, FF, 768, mask_s, lambda c, acc: p_d.put(acc.astype(bf16), off=c))
    us[8] = us[7]
    arrive()

    for g in range(4):
        rows = pl.ds(g * GR, GR)
        tb = dg(onehot(to_frames(g), R), rcv_b[...], 1, 0)
        x1[rows, :] = a0[rows, :].astype(f32) + tb
    norm(1, lambda rows: x1[rows, :], lambda rows, v: p_o2.put(v, rows))
    loads["q1"].wait()
    forward(3, p_o2, wq.at[1], QKV, 768, mask_s, lambda c, acc: p_qkv2.put(acc.astype(bf16), off=c))
    spatial_loop(lambda rows, n, off, bias: attend_pair(p_qkv2, rows, n, off, bias, p_o2))
    loads["p2"].wait()

    def add_spatial(c, acc):
        x2[:, cols(c, 384)] = x1[:, cols(c, 384)] + acc

    forward(4, p_o2, wp.at[2], D, 384, mask_s, add_spatial)

    norm(2, lambda rows: x2[rows, :], lambda rows, v: p_a0.put(v, rows))
    loads["i"].wait()

    def activate(c, acc):
        tmp_w = acc.shape[1]
        tmp[:, pl.ds(0, tmp_w)] = acc
        @pl.loop(0, R // 32)
        def _(i):
            rows = pl.ds(pl.multiple_of(i * 32, 32), 32)
            v = tmp[rows, pl.ds(0, tmp_w)]
            phi, e = normal_parts(v)
            slope = phi + v * e * 0.3989422804014327
            p_g.put((v * phi).astype(bf16), rows, c)
            p_d.put((p_d.get(rows, c, tmp_w).astype(f32) * slope).astype(bf16), rows, c)

    forward(5, p_a0, wi, FF, 768, mask_s, activate)

    def emit_out(c, acc):
        y = (x2[:, cols(c, 384)] + acc).astype(bf16)
        for g in range(4):
            out[g // 2, g % 2, :, cols(c, 384)] = y[g * GR : g * GR + NP]

    forward(6, p_g, wo, D, 384, mask_s, emit_out)
    us[7] = us[8]
    adapter_grads(6, p_g, p_a1)

    def emit_tmp(c, acc):
        tmp[:, cols(c, 384)] = acc

    backward(5, p_d, wi, D, 384, mask_s, emit_tmp)
    adapter_grads(5, p_a0, p_d)
    loads_back = [pltpu.make_async_copy(spill.at[i], b, psem.at[i]) for i, b in enumerate((buf_g, buf_d))]
    for cp in loads_back:
        cp.start()

    def step_two(rows):
        dx = a1[rows, :].astype(f32) + norm_back_rows(x2[rows, :], gain(2), tmp[rows, :])
        x2[rows, :] = dx
        a0[rows, :] = dx.astype(bf16)

    chunks(64, step_two)

    backward(4, p_a0, wp.at[2], D, 384, mask_s, lambda c, acc: p_a1.put(acc.astype(bf16), off=c))
    adapter_grads(4, p_o2, p_a0)
    spatial_loop(lambda rows, n, off, bias: attend_pair_back(p_qkv2, rows, n, off, bias, p_a1))
    backward(3, p_qkv2, wq.at[1], D, 384, mask_s, emit_tmp)

    def step_one(rows):
        dx = x2[rows, :] + norm_back_rows(x1[rows, :], gain(1), tmp[rows, :])
        x2[rows, :] = dx
        a0[rows, :] = dx.astype(bf16)

    chunks(64, step_one)
    arrive = exchange(2, p_a0, to_message, rcv_a)
    norm(1, lambda rows: x1[rows, :], lambda rows, v: p_a1.put(v, rows))
    adapter_grads(3, p_a1, p_qkv2)
    for cp in loads_back:
        cp.wait()
    arrive()

    for i in range(4):
        p_a0.put(dg(onehot(to_patches(i), R), rcv_a[...], 1, 0).astype(bf16), pl.ds(i * GR, GR))
    backward(2, p_a0, wp.at[1], D, 384, mask_t, lambda c, acc: p_a1.put(acc.astype(bf16), off=c))
    adapter_grads(2, m1, p_a0)
    backward(1, p_a1, wp.at[0], D, 384, mask_t, lambda c, acc: spare.put(acc.astype(bf16), off=c))
    adapter_grads(1, o1, p_a1)
    temporal_loop(lambda rows, n, off, bias: attend_pair_back(qkv1, rows, n, off, bias, spare))
    backward(0, qkv1, wq.at[0], D, 384, mask_t, emit_tmp)

    def step_zero(rows):
        dx = norm_back_rows(xt.get(rows).astype(f32), gain(0), tmp[rows, :])
        a0[rows, :] = dx.astype(bf16)

    chunks(64, step_zero)
    arrive = exchange(3, p_a0, from_patches, rcv_b)
    adapter_grads(0, h1, qkv1)
    arrive()
    for g in range(4):
        dxt = dg(onehot(to_frames(g), R), rcv_b[...], 1, 0)
        total = x2[pl.ds(g * GR, GR), :] + dxt
        ig[g // 2, g % 2] = total.astype(bf16)[:NP]


def layer(x, g, ad, nm, hq, hp, hi, ho):
    vm = pl.BlockSpec(memory_space=pltpu.VMEM)
    hbm = pl.BlockSpec(memory_space=pl.ANY)
    dma = pltpu.SemaphoreType.DMA
    rows = lambda w, t=bf16: pltpu.VMEM((R, w), t)
    return pl.pallas_call(
        layer_kernel,
        out_shape=[
            jax.ShapeDtypeStruct(x.shape, bf16),
            jax.ShapeDtypeStruct(x.shape, bf16),
            jax.ShapeDtypeStruct((32, ADW), bf16),
            jax.ShapeDtypeStruct((2, R, FF), bf16),
        ],
        in_specs=[vm] * 4 + [hbm] * 4,
        out_specs=[vm] * 3 + [hbm],
        scratch_shapes=[
            pltpu.VMEM((2, D, QKV), bf16), pltpu.VMEM((3, D, D), bf16), pltpu.VMEM((D, FF), bf16), pltpu.VMEM((FF, D), bf16),
            pltpu.VMEM((3 * GR, D), bf16), rows(D), rows(D), rows(FF), rows(FF), rows(D, f32), rows(D, f32), rows(D, f32),
            rows(D), rows(QKV), rows(D), rows(D), pltpu.VMEM((9, R, 32), bf16),
            dma((7,)), dma((4, 3)), dma((4, 3)), dma((2,)),
        ],
        compiler_params=pltpu.CompilerParams(
            collective_id=1, has_side_effects=True, vmem_limit_bytes=64 * 2**20 - 2**17
        ),
        name="layer",
    )(x, g, ad, nm, hq, hp, hi, ho)


class Many:
    def __init__(self, cps):
        self.cps = cps

    def start(self):
        for cp in self.cps:
            cp.start()

    def wait_recv(self):
        for cp in self.cps:
            cp.wait_recv()

    def wait_send(self):
        for cp in self.cps:
            cp.wait_send()


def column_groups(a, lead, rows, total, width):
    return [(a, lead, 0, rows, c, width) for c in range(0, total, width)]


GROUPS = (
    [(4, None, 0, 96, 0, 1664), (4, None, 0, 96, 1664, 1536)]
    + column_groups(0, 0, 96, QKV, D)
    + [(1, 0, 0, 96, 0, D), (1, 1, 0, 96, 0, D)]
    + column_groups(0, 1, 96, QKV, D)
    + [(1, 2, 0, 96, 0, D)]
    + column_groups(2, None, 96, FF, D)
    + [(3, None, r, 96, 0, D) for r in range(0, 384, 96)]
)


def gather_kernel(n_in, *refs):
    ahead, lag = 3, 1
    groups = GROUPS
    ins = refs[:n_in]
    outs = refs[n_in : 2 * n_in]
    zs, zr, ys, yr, xs, xr, cs, cr, ls = refs[2 * n_in :]
    clip = lax.axis_index("clip")
    frame = lax.axis_index("frame")
    z, y, x, c = clip // 2, clip % 2, frame // 2, frame % 2

    def dev(zz, yy, xx, cc):
        return {"clip": zz * 2 + yy, "frame": xx * 2 + cc}

    zpeers = [lax.rem(z + k, 4) for k in (1, 2, 3)]
    ypeer, xpeer, cpeer = dev(z, 1 - y, x, c), dev(z, y, 1 - x, c), dev(z, y, x, 1 - c)
    barrier = pltpu.get_barrier_semaphore()
    for p in [dev(zz, y, x, c) for zz in zpeers] + [ypeer, xpeer, cpeer]:
        pl.semaphore_signal(barrier, inc=1, device_id=p, device_id_type=MESH)
    pl.semaphore_wait(barrier, 6)

    def src(g, off, n):
        a, lead, r0, rows, c0, width = groups[g]
        r = ins[a] if lead is None else ins[a].at[lead]
        return r.at[pl.ds(r0 + off, n), pl.ds(c0, width)]

    def dst(g, zz, yy, off, n):
        a, lead, r0, rows, c0, width = groups[g]
        r = outs[a] if lead is None else outs[a].at[lead]
        return r.at[zz, yy, pl.ds(r0 + off, n), pl.ds(c0, width)]

    def remote(s, d, ss, rs, p):
        return pltpu.make_async_remote_copy(
            src_ref=s, dst_ref=d, send_sem=ss, recv_sem=rs, device_id=p, device_id_type=MESH
        )

    def same(ref, ss, rs, p):
        return remote(ref, ref, ss, rs, p)

    ng = len(groups)
    local = []
    moved = {k: {} for k in ("z", "y", "x1", "x2", "c1", "c2")}
    for a in range(n_in):
        r, d = ins[a], outs[a]
        for s, t in (
            [(r.at[k], d.at[k, z, y]) for k in range(r.shape[0])]
            if len(r.shape) == 3
            else [(r, d.at[z, y])]
        ):
            local.append(pltpu.make_async_copy(s, t, ls.at[len(local)]))
    for cp in local:
        cp.start()
    two = pl.multiple_of(16 * (3 * c + x), 16)
    one = pl.multiple_of(16 * (3 * c + 2 * x), 16)
    half = pl.multiple_of(48 * c, 16)

    def start(kind, g, cps):
        moved[kind][g] = Many(cps)
        moved[kind][g].start()

    def start_z(g):
        start(
            "z",
            g,
            [
                remote(src(g, two, 32), dst(g, z, y, two, 32), zs.at[g, k], zr.at[g, k], dev(zpeers[k], y, x, c))
                for k in range(3)
            ],
        )

    def start_y(g):
        start("y", g, [same(dst(g, q, y, two, 32), ys.at[g, q], yr.at[g, q], ypeer) for q in range(4)])
        start(
            "x1",
            g,
            [same(dst(g, lax.rem(z + q, 4), y, one, 16), xs.at[g, 0, q], xr.at[g, 0, q], xpeer) for q in (1, 2, 3)],
        )

    def start_x(g):
        start("x2", g, [same(dst(g, q, 1 - y, one, 16), xs.at[g, 1, q], xr.at[g, 1, q], xpeer) for q in range(4)])

    def start_c(g, k):
        yy = y if k == 0 else 1 - y
        start(
            ("c1", "c2")[k],
            g,
            [
                same(dst(g, lax.rem(z + q, 4), yy, half, 48), cs.at[g, k, q], cr.at[g, k, q], cpeer)
                for q in range(1 - k, 4)
            ],
        )

    for g in range(min(ahead, ng)):
        start_z(g)
    for cp in local:
        cp.wait()
    for s in range(ng + 3 * lag):
        if s < ng:
            moved["z"][s].wait_recv()
            if s + ahead < ng:
                start_z(s + ahead)
            start_y(s)
        g = s - lag
        if 0 <= g < ng:
            moved["y"][g].wait_recv()
            start_x(g)
            moved["x1"][g].wait_recv()
            start_c(g, 0)
        g = s - 2 * lag
        if 0 <= g < ng:
            moved["x2"][g].wait_recv()
            start_c(g, 1)
        g = s - 3 * lag
        if 0 <= g < ng:
            moved["c1"][g].wait_recv()
            moved["c2"][g].wait_recv()
    for kind in moved.values():
        for m in kind.values():
            m.wait_send()


def gather(arrays):
    n, ng = len(arrays), len(GROUPS)
    shapes = []
    for a in arrays:
        lead = a.ndim == 3
        shapes.append((a.shape[0], 4, 2) + a.shape[1:] if lead else (4, 2) + a.shape)
    dma = pltpu.SemaphoreType.DMA
    return pl.pallas_call(
        functools.partial(gather_kernel, n),
        out_shape=[jax.ShapeDtypeStruct(s, a.dtype) for s, a in zip(shapes, arrays)],
        in_specs=[pl.BlockSpec(memory_space=pl.ANY)] * n,
        out_specs=[pl.BlockSpec(memory_space=pltpu.VMEM)] * n,
        scratch_shapes=[
            dma((ng, 3)), dma((ng, 3)), dma((ng, 4)), dma((ng, 4)),
            dma((ng, 2, 4)), dma((ng, 2, 4)), dma((ng, 2, 4)), dma((ng, 2, 4)), dma((8,)),
        ],
        compiler_params=pltpu.CompilerParams(
            collective_id=0, has_side_effects=True, vmem_limit_bytes=48 * 2**20
        ),
        name="gather",
    )(*arrays)


def piece_widths(w):
    return [w] * 6 + [4 * w] + [3 * w] * 2 + [w] * 4 + [4 * w]


def pack_adapters(adapt_down, adapt_down_wide, adapt_up_qkv, adapt_up, adapt_up_wide):
    adapters = adapt_down_wide.shape[0]

    def flat(v):
        return v.reshape(adapters, RANK, -1)

    return jnp.concatenate(
        [
            flat(adapt_down.transpose(1, 3, 0, 2)),
            flat(adapt_down_wide.transpose(0, 2, 1)),
            flat(adapt_up_qkv.transpose(1, 2, 0, 3)),
            flat(adapt_up.transpose(1, 2, 0, 3)),
            flat(adapt_up_wide),
        ],
        axis=-1,
    )


def join_pieces(parts, w):
    joined, at = [], 0
    for width in piece_widths(w):
        piece = parts[:, :, at : at + width]
        joined.append(piece.transpose(1, 0, 2).reshape(parts.shape[1], -1))
        at += width
    return jnp.concatenate(joined, axis=-1)


def split_pieces(rows, w, owners):
    parts, at = [], 0
    for width in piece_widths(w):
        piece = rows[:, at : at + width * owners]
        parts.append(piece.reshape(rows.shape[0], owners, width).transpose(1, 0, 2))
        at += width * owners
    return jnp.concatenate(parts, axis=-1)


def per_device(
    inputs,
    out_grad,
    adapter_index,
    norm_gain,
    norm_bias,
    qkv_weight,
    proj_weight,
    mlp_in,
    mlp_out,
    adapt_down,
    adapt_down_wide,
    adapt_up_qkv,
    adapt_up,
    adapt_up_wide,
):
    owners = lax.axis_size("clip")
    adapters = adapt_down_wide.shape[0]
    clips = inputs.shape[0]
    w = norm_gain.shape[1]
    packed = pack_adapters(adapt_down, adapt_down_wide, adapt_up_qkv, adapt_up, adapt_up_wide)
    norms = jnp.concatenate([norm_gain, norm_bias], axis=0)
    if owners == 8:
        small = jnp.concatenate(
            [packed.reshape(96, -1), jnp.pad(norms, ((0, 90), (0, 128 - w)))], axis=1
        )
        full_qkv, full_proj, full_in, full_out, table = gather(
            (qkv_weight, proj_weight, mlp_in, mlp_out, small)
        )
        full_qkv = full_qkv.reshape(2, D, QKV)
        full_proj = full_proj.reshape(3, D, D)
        full_in = full_in.reshape(D, FF)
        full_out = full_out.reshape(FF, D)
        table = table.reshape(owners, 96, -1)
        all_norms = table[:, :6, -128:][:, :, :w]
        table = table[:, :, :-128].reshape(owners, adapters, RANK, 24 * w)
    else:
        full_qkv = lax.all_gather(qkv_weight, "clip", axis=1, tiled=True)
        full_proj = lax.all_gather(proj_weight, "clip", axis=1, tiled=True)
        full_in = lax.all_gather(mlp_in, "clip", axis=0, tiled=True)
        full_out = lax.all_gather(mlp_out, "clip", axis=0, tiled=True)
        table = lax.all_gather(packed, "clip", axis=0)
        all_norms = lax.all_gather(norms, "clip", axis=0)
    nm = jnp.pad(all_norms.transpose(1, 0, 2).reshape(6, D).astype(f32), ((0, 2), (0, 0)))
    chosen = jnp.take(table, adapter_index, axis=1).reshape(owners, clips * RANK, 24 * w)
    ad = join_pieces(chosen, w)
    output, input_grad, grads, _ = layer(
        inputs, out_grad, ad, nm, full_qkv, full_proj, full_in, full_out
    )
    parts = split_pieces(grads, w, owners)
    parts = lax.all_to_all(parts, "clip", split_axis=0, concat_axis=0, tiled=True)
    every = lax.all_gather(adapter_index, "clip", axis=0, tiled=True)
    pick = (every[:, None] == jnp.arange(adapters, dtype=jnp.int32)[None, :]).astype(bf16)
    summed = jnp.einsum(
        "ca,crm->arm", pick, parts.reshape(owners * clips, RANK, 24 * w), preferred_element_type=f32
    )
    summed = lax.psum(summed.astype(bf16), "frame").astype(f32)
    return (output, input_grad) + unpack_grads(summed, w)


def unpack_grads(summed, w):
    adapters = summed.shape[0]
    down = summed[:, :, : 6 * w].reshape(adapters, RANK, 6, w).transpose(2, 0, 3, 1)
    down_wide = summed[:, :, 6 * w : 10 * w].transpose(0, 2, 1)
    up_qkv = summed[:, :, 10 * w : 16 * w].reshape(adapters, RANK, 2, 3 * w).transpose(2, 0, 1, 3)
    up = summed[:, :, 16 * w : 20 * w].reshape(adapters, RANK, 4, w).transpose(2, 0, 1, 3)
    return (down, down_wide, up_qkv, up, summed[:, :, 20 * w :])


def solution(mesh):
    return jax.shard_map(
        per_device,
        mesh=mesh,
        in_specs=(
            P("clip", "frame", None, None),
            P("clip", "frame", None, None),
            P("clip"),
            P(None, "clip"),
            P(None, "clip"),
            P(None, "clip", None),
            P(None, "clip", None),
            P("clip", None),
            P("clip", None),
            P(None, None, "clip", None),
            P(None, "clip", None),
            P(None, None, None, "clip"),
            P(None, None, None, "clip"),
            P(None, None, "clip"),
        ),
        out_specs=(
            P("clip", "frame", None, None),
            P("clip", "frame", None, None),
            P(None, None, "clip", None),
            P(None, "clip", None),
            P(None, None, None, "clip"),
            P(None, None, None, "clip"),
            P(None, None, "clip"),
        ),
        check_vma=False,
    )
```

time: 1390 us -> 542 us (0.39)
  Pallas kernels: 0 us -> 392 us
  local copies, waits for them, and re-layouts: 407 us -> 55.8 us
  blocking collectives: 297 us -> 28.8 us
  waiting for transfers between devices: 287 us -> 28 us
  matrix products: 198 us -> 1.32 us
  other arithmetic: 166 us -> 3.37 us
    pallas_call x0 -> x2, Pallas kernels: none -> 392 us  [the longest x1 262 us: layer(): pl.pallas_call(layer_kernel, out_shape=[jax.ShapeDtypeStruct(x.shape, bf1...]
    all_gather x5 -> x0, blocking collectives: 278 us -> none  [the longest x1 167 us: per_device(): lax.all_gather(adapt_up, 'clip', axis=3, tiled=True)]
    all_gather x6 -> x0, waiting for transfers between devices: 226 us -> none  [the longest x1 97.5 us: per_device(): lax.all_gather(qkv_weight, 'clip', axis=1, tiled=True)]
    dot_general x87 -> x1, matrix products: 198 us -> 1.32 us  [per_device(): jnp.einsum('ca,crm->arm', pick, parts.reshape(owners * clips, RANK, 24 *...]
    unnamed x275 -> x57, local copies, waits for them, and re-layouts: 209 us -> 18.5 us
    convert_element_type x17 -> x1, other arithmetic: 69.9 us -> 0.08 us  [per_device(): summed = lax.psum(summed.astype(bf16), 'frame').astype(f32)]
    convert_element_type x16 -> x1, local copies, waits for them, and re-layouts: 57.4 us -> 0.09 us  [per_device(): all_norms.transpose(1, 0, 2).reshape(6, D).astype(f32)]
    reshape x16 -> x36, local copies, waits for them, and re-layouts: 69.1 us -> 16 us  [the longest x1 8.53 us: per_device(): table = table[:, :, :-128].reshape(owners, adapters, RANK, 24 * w)]
  transfers between devices with their start and end apart: 15 -> 2, of which waited for: 6 -> 1; matrix products, arithmetic and copies ran while one was open for 39% -> 1% of each run, Pallas kernels for 0% -> 0%
where the time goes in v1:
time: 542 us; the launch traced here: 532 us
  Pallas kernels  392 us (72%)
  local copies, waits for them, and re-layouts  55.8 us (10%)
  blocking collectives  28.8 us (5%)
  waiting for transfers between devices  28 us (5%)
  between operations  15.5 us (3%)
  starting transfers between devices  7.72 us (1%)
    pallas_call x1, Pallas kernels, layer(): pl.pallas_call(layer_kernel, out_shape=[jax.ShapeDtypeStruct(x.shape, bf1...  262 us
    pallas_call x1, Pallas kernels, gather(): pl.pallas_call(functools.partial(gather_kernel, n), out_shape=[jax.ShapeD...  130 us
    unnamed x1, blocking collectives  28.8 us
    psum x1, waiting for transfers between devices, per_device(): summed = lax.psum(summed.astype(bf16), 'frame').astype(f32)  28 us
    unnamed x57, local copies, waits for them, and re-layouts  18.5 us
  transfers between devices with their start and end apart: 2, of which 1 were waited for; matrix products, arithmetic and copies ran while one was open for 1% of the time, Pallas kernels for 0%

profile of v1, /device:TPU:0, one launch (start us, length us, event | category | flops | bytes accessed | tf_op | source)
XLA Modules:
  0.0 532.5 jit_solution(6090190203086997951)
XLA Ops:
  7.2 0.7 compare_select_fusion
  7.9 0.7 compare_and_fusion
  8.6 1.1 copy.60
  9.6 0.2 reshape.152
  9.8 1.1 copy.61
  11.0 0.2 reshape.153
  11.2 0.1 reshape.154
  11.4 0.4 concatenate.15
  11.9 1.3 reshape.155
  13.2 1.1 pad_maximum_fusion.refs_4_
  14.4 130.1 %gather.11 = (bf16[2,4,2,96,2304]{4,3,2,1,0:T(8,128)(2,1)}, bf16[3,4,2,96,768]{4,3,2,1,0:T(8,128)(2,1)}, bf16[4,2,96,3072]{3,2,1,0:T(8,128)(2,1)}, bf16[4,2,384,...) custom-call(bf16[2,96,2304]{2,1,0:T(8,128)(2,1)S(1)} %copy-done, bf16[3,96,768]{2,1,0:T(8,128)(2,1)S(1)} %copy-done.3, ...), custom_call_target="tpu_custom_call" | custom-call | tf_op jit(solution)/shard_map/gather/pallas_call | solution.py:601
  144.5 4.9 slice.144
  149.3 8.5 %reshape.157 = bf16[8,8,16,2304]{3,2,1,0:T(8,128)(2,1)} reshape(bf16[8,96,3072]{2,1,0:T(8,128)(2,1)} %slice.144) | data formatting | bytes 9437184 | tf_op jit(solution)/shard_map/reshape | solution.py:692
  157.9 3.0 gather_fusion
  161.1 0.2 bitcast_select_fusion
  161.3 0.2 slice_bitcast_fusion.5
  161.5 0.1 slice_bitcast_fusion.1
  161.6 0.2 slice_bitcast_fusion.2
  161.8 0.7 slice.159
  162.7 0.6 constant_dynamic-update-slice_fusion.13
  164.2 0.2 reshape.165
  164.4 0.2 reshape.166
  165.3 0.6 pad_convert_fusion.nm
  165.9 1.1 copy.79.x_ref
  167.1 0.6 copy-done.8
  167.7 1.2 copy.80.g_ref
  168.9 0.6 constant_dynamic-update-slice_fusion.12
  169.5 0.6 constant_dynamic-update-slice_fusion.11
  170.1 0.6 constant_dynamic-update-slice_fusion.10
  170.7 0.6 constant_dynamic-update-slice_fusion.9
  171.4 0.6 constant_dynamic-update-slice_fusion.8
  172.0 0.7 constant_dynamic-update-slice_fusion.7
  172.7 0.7 constant_dynamic-update-slice_fusion.6
  173.3 0.7 constant_dynamic-update-slice_fusion.5
  174.0 0.6 constant_dynamic-update-slice_fusion.4
  174.6 0.6 constant_dynamic-update-slice_fusion.3
  175.3 0.6 constant_dynamic-update-slice_fusion.2
  175.9 0.6 constant_dynamic-update-slice_fusion.1
  176.5 0.7 constant_dynamic-update-slice_fusion.ad
  177.2 261.9 %layer.1 = (bf16[2,2,196,768]{3,2,1,0:T(8,128)(2,1)}, bf16[2,2,196,768]{3,2,1,0:T(8,128)(2,1)}, bf16[32,18432]{1,0:T(8,128)(2,1)}, bf16[2,832,3072]{2,1,0:T(8,128)(2,1)}) custom-call(bf16[2,2,196,768]{3,2,1,0:T(8,128)(2,1)} %copy.79.x_ref, bf16[2,2,196,768]{3,2,1,0:T(8,128)(2,1)} %copy.80.g_ref, bf16[32,18432]{1,0:T(8,128)(2,1)} %constant_dynamic-update-slice_fusion.ad, ...), custom_call_target="tpu_custom_call" | custom-call | tf_op jit(solution)/shard_map/layer/pallas_call | solution.py:419
  439.1 1.1 fusion.11
  440.2 1.0 fusion.12
  441.2 1.1 fusion.10
  442.2 0.1 reshape.187
  442.7 0.3 reshape.183
  443.0 0.3 reshape.184
  444.4 3.5 concatenate.19
  447.9 7.7 %all-to-all-start = ((bf16[8,32,2304]{2,1,0:T(8,128)(2,1)}), bf16[8,32,2304]{2,1,0:T(8,128)(2,1)S(1)}, u32[]{:S(2)}, u32[]{:S(2)}) async-start(bf16[8,32,2304]{2,1,0:T(8,128)(2,1)} %concatenate.19), calls=%async_computation | async-start | bytes 2359296 | tf_op jit(solution)/shard_map/all_to_all | solution.py:707
  455.6 0.6 dynamic-slice
  456.9 0.4 dynamic-update-slice
  457.3 28.8 %all-reduce.2 = s32[16]{0:T(128)S(1)} all-reduce(s32[16]{0:T(128)S(1)} %dynamic-update-slice), channel_id=1, replica_groups=mesh['clip'=8,'frame'=4] {'clip'}, use_global_device_ids=true, to_apply=%add.2 | all-reduce | flops 16 | bytes 128
  486.1 1.3 convolution_convert_fusion
  487.5 1.9 copy.100
  489.4 1.9 copy.99
  491.4 28.0 %all-reduce.5.cloned.1.call-done = bf16[8,16,2304]{2,0,1:T(8,128)(2,1)} async-done(((bf16[8,16,2304]{2,0,1:T(8,128)(2,1)}), bf16[8,16,2304]{2,0,1:T(8,128)(2,1)}) %all-reduce.5.cloned.1.call-update) | async-done | bytes 589840 | tf_op jit(solution)/shard_map/psum | solution.py:713
  519.3 1.1 fusion.14
  520.6 0.2 reshape.191
  520.7 0.8 copy.101
  521.8 0.7 copy.102
  522.5 0.3 reshape.192
  522.8 0.9 copy.128
  523.7 0.2 reshape.193
  523.9 0.9 copy.129
  524.7 0.7 copy.103
  (87 shorter events, 3.7 us)
Async XLA Ops:
  7.2 3.9 copy-start.9
  7.2 4.2 copy-start.10
  7.2 4.2 copy-start.11
  11.4 1.8 copy-start.12
  11.4 1.8 copy-start.13
  11.4 2.9 copy-start.3
  11.8 2.5 copy-start
  11.9 2.5 copy-start.1
  11.9 2.5 copy-start.2
  164.3 1.6 copy-start.7
  165.9 1.7 copy-start.8
  447.9 7.7 %copy-start.15 = (u32[32]{0:T(128)S(1)}, u32[32]{0:T(128)}, u32[]{:S(2)}) copy-start(u32[32]{0:T(128)} %constant.30) | copy-start | bytes 388
  447.9 9.0 %copy-start.14 = (s32[2]{0:T(128)S(1)}, s32[2]{0:T(128)}, u32[]{:S(2)}) copy-start(s32[2]{0:T(128)} %param.16) | copy-start | bytes 28
  447.9 38.2 %all-to-all-start = ((bf16[8,32,2304]{2,1,0:T(8,128)(2,1)}), bf16[8,32,2304]{2,1,0:T(8,128)(2,1)S(1)}, u32[]{:S(2)}, u32[]{:S(2)}) async-start(bf16[8,32,2304]{2,1,0:T(8,128)(2,1)} %concatenate.19), calls=%async_computation | async-start | bytes 2359296 | tf_op jit(solution)/shard_map/all_to_all | solution.py:707
  455.6 63.8 %all-reduce.5.cloned.1.call-start = ((), (), s32[]{:S(2)}) async-start(), calls=%async_computation.1 | async-start | bytes 1179648 | tf_op jit(solution)/shard_map/psum | solution.py:713
  486.1 1.3 copy-start.6
  487.4 2.0 copy-start.5
  520.5 1.1 copy-start.4
Sparse Core Ops, SparseCore 0:
  487.6 31.7 all-reduce.4

commit v2 on v1

v2 whole, which is shorter than its diff:
```python
import functools
import jax
import jax.numpy as jnp
from jax import lax
from jax.experimental import pallas as pl
from jax.experimental.pallas import tpu as pltpu
from jax.sharding import PartitionSpec as P

EPS = 1e-06
MESH = pl.DeviceIdType.MESH
f32 = jnp.float32
bf16 = jnp.bfloat16
D, FF, QKV, RANK = 768, 3072, 2304, 16
NP, GR, R = 196, 208, 832
DOWN = (0, 768, 1536, 2304, 3072, 3840, 4608)
UP = (7680, 12288, 13056, 9984, 13824, 15360, 14592)
ADW = 18432
BIG = 1e30


def dg(a, b, ca, cb):
    return lax.dot_general(a, b, (((ca,), (cb,)), ((), ())), preferred_element_type=f32)


def iota(shape, d):
    return lax.broadcasted_iota(jnp.int32, shape, d)


def cols(off, w):
    return pl.ds(off if isinstance(off, int) else pl.multiple_of(off, 128), w)


def normal_parts(v):
    e = jnp.exp(-0.5 * v * v)
    t = 1.0 / (1.0 + 0.2316419 * jnp.abs(v))
    poly = t * (
        0.127414796
        + t * (-0.142248368 + t * (0.7107068705 + t * (-0.7265760135 + t * 0.5307027145)))
    )
    tail = poly * e
    return jnp.where(v >= 0, 1.0 - tail, tail), e


def onehot(col, width):
    return jnp.where(iota((col.shape[0], width), 1) == col, 1.0, 0.0).astype(bf16)


def message_rows():
    m = iota((GR, 1), 0)
    c = jnp.where(m >= 98, 1, 0)
    rest = m - 98 * c
    f = jnp.where(rest >= 49, 1, 0)
    return m < 196, c, f, rest - 49 * f


def to_message(owner):
    ok, c, f, q = message_rows()
    return jnp.where(ok, (2 * c + f) * GR + 49 * owner + q, -1)


def from_patches(owner):
    ok, c, f, q = message_rows()
    return jnp.where(ok, 392 * c + 8 * q + 2 * owner + f, -1)


def to_patches(chunk):
    t = iota((GR, 1), 0) + chunk * GR
    c = jnp.where(t >= 392, 1, 0)
    u = t - 392 * c
    q, fr = u >> 3, u & 7
    return jnp.where(t < 784, (fr >> 1) * GR + c * 98 + (fr & 1) * 49 + q, -1)


def to_frames(g):
    p = iota((GR, 1), 0)
    d = jnp.where(p >= 49, 1, 0) + jnp.where(p >= 98, 1, 0) + jnp.where(p >= 147, 1, 0)
    return jnp.where(p < NP, d * GR + (g // 2) * 98 + (g % 2) * 49 + p - 49 * d, -1)


def clip_mask(first):
    return (iota((R, 32), 0) >= first) == (iota((R, 32), 1) >= 16)


class Part:
    def __init__(self, ref, c0, width):
        self.ref, self.c0, self.width = ref, c0, width

    def get(self, rows=slice(None), off=0, width=None):
        return self.ref[rows, cols(self.c0 + off, self.width if width is None else width)]

    def put(self, val, rows=slice(None), off=0):
        self.ref[rows, cols(self.c0 + off, val.shape[1])] = val


def chunks(size, body):
    @pl.loop(0, R // size)
    def _(i):
        body(pl.ds(pl.multiple_of(i * size, size), size))


def tiles(total, tile, body, between):
    if total == tile:
        body(0)
    elif between is None:

        @pl.loop(0, total // tile)
        def _(i):
            body(i * tile)

    else:
        for c in range(0, total, tile):
            body(c)
            if c + tile < total:
                between()


def norm_rows(v):
    mean = jnp.mean(v, axis=-1, keepdims=True)
    cen = v - mean
    rstd = lax.rsqrt(jnp.mean(cen * cen, axis=-1, keepdims=True) + EPS)
    return cen * rstd, rstd


def norm_back_rows(v, gain, dh):
    hat, rstd = norm_rows(v)
    g = dh * gain
    m1 = jnp.mean(g, axis=-1, keepdims=True)
    m2 = jnp.mean(g * hat, axis=-1, keepdims=True)
    return rstd * (g - m1 - hat * m2)


def head_masks(n):
    first = iota((n, 128), 1) < 64
    one, zero = jnp.ones((n, 128), bf16), jnp.zeros((n, 128), bf16)
    return jnp.where(first, one, zero), jnp.where(first, zero, one)


def eye(n):
    return jnp.where(iota((n, n), 0) == iota((n, n), 1), 1.0, 0.0).astype(bf16)


def attend_pair(qkv, rows, n, off, bias, out):
    q = qkv.get(rows, off, 128)
    k = qkv.get(rows, D + off, 128)
    v_t = dg(eye(128), qkv.get(rows, 2 * D + off, 128), 1, 1).astype(bf16)
    parts = []
    for h, hm in enumerate(head_masks(n)):
        s = dg(k * (hm * 0.125).astype(bf16), q, 1, 1) + bias
        p = jnp.exp(s - jnp.max(s, axis=0, keepdims=True))
        total = jnp.sum(p, axis=0, keepdims=True)
        parts.append(dg(v_t[64 * h : 64 * h + 64], p.astype(bf16), 1, 0) * (1.0 / total))
    o_t = jnp.concatenate(parts, axis=0).astype(bf16)
    out.put(dg(eye(n), o_t, 1, 1).astype(bf16), rows, off)


def attend_pair_back(qkv, rows, n, off, bias, dout):
    q = qkv.get(rows, off, 128)
    k = qkv.get(rows, D + off, 128)
    v = qkv.get(rows, 2 * D + off, 128)
    do = dout.get(rows, off, 128)
    k_t = (dg(eye(128), k, 1, 1) * 0.125).astype(bf16)
    dq_t, dks, dvs = [], [], []
    for h, hm in enumerate(head_masks(n)):
        s = dg(k * (hm * 0.125).astype(bf16), q, 1, 1) + bias
        p = jnp.exp(s - jnp.max(s, axis=0, keepdims=True))
        p = p * (1.0 / jnp.sum(p, axis=0, keepdims=True))
        dp = dg(v * hm, do, 1, 1)
        dvs.append(dg(p.astype(bf16), do, 1, 0))
        ds = (p * (dp - jnp.sum(dp * p, axis=0, keepdims=True))).astype(bf16)
        dq_t.append(dg(k_t[64 * h : 64 * h + 64], ds, 1, 0))
        dks.append(dg(ds, q, 1, 0))
    first = iota((n, 128), 1) < 64
    dq = dg(eye(n), jnp.concatenate(dq_t, axis=0).astype(bf16), 1, 1)
    qkv.put(dq.astype(bf16), rows, off)
    qkv.put((jnp.where(first, dks[0], dks[1]) * 0.125).astype(bf16), rows, D + off)
    qkv.put(jnp.where(first, dvs[0], dvs[1]).astype(bf16), rows, 2 * D + off)


def spatial_loop(body, between=None):
    bias = jnp.where(iota((GR, 1), 0) < NP, 0.0, -BIG)

    def group(g):
        @pl.loop(0, 6)
        def _(i):
            body(pl.ds(g * GR if isinstance(g, int) else pl.multiple_of(g * GR, 16), GR), GR, i * 128, bias)

    if between is None:
        pl.loop(0, 4)(group)
    else:
        for g in range(4):
            group(g)
            between()


def temporal_loop(body, between=None):
    def bias(n):
        return jnp.where((iota((n, n), 0) >> 3) == (iota((n, n), 1) >> 3), 0.0, -BIG)

    def block(i, n):
        rows = pl.ds(i * 128 if isinstance(i, int) else pl.multiple_of(i * 128, 128), n)
        for u in range(6):
            body(rows, n, u * 128, bias(n))

    if between is None:
        pl.loop(0, 6)(lambda i: block(i, 128))
    else:
        for k in range(3):
            pl.loop(2 * k, 2 * k + 2)(lambda i: block(i, 128))
            between()
    block(6, 64)


class Many:
    def __init__(self, cps):
        self.cps = cps
        for cp in cps:
            cp.start()

    def wait_recv(self):
        for cp in self.cps:
            cp.wait_recv()

    def wait_send(self):
        for cp in self.cps:
            cp.wait_send()


def gather_groups():
    out = [("ad", "table", None, 32 * k, 32, 0, 0, FF) for k in range(4)]
    out += [("q0", "q", 0, 0, 96, 16, c, D) for c in range(0, QKV, D)]
    out += [("p0", "p", 0, 0, 96, 16, 0, D), ("p1", "p", 1, 0, 96, 16, 0, D)]
    out += [("q1", "q", 1, 0, 96, 16, c, D) for c in range(0, QKV, D)]
    out += [("p2", "p", 2, 0, 96, 16, 0, D)]
    out += [("o", "o", None, r, 96, 16, 0, D) for r in range(0, 384, 96)]
    out += [("i", "i", None, 0, 96, 16, c, D) for c in range(0, FF, D)]
    return out


class Gather:
    def __init__(self, srcs, dsts, sems, local, ahead=3, lag=1):
        self.groups = gather_groups()
        self.srcs, self.dsts, self.sems = srcs, dsts, sems
        self.ahead, self.lag = ahead, lag
        clip, frame = lax.axis_index("clip"), lax.axis_index("frame")
        self.z, self.y, self.x, self.c = clip // 2, clip % 2, frame // 2, frame % 2
        z, y, x, c = self.z, self.y, self.x, self.c
        self.zpeers = [self.dev(lax.rem(z + k, 4), y, x, c) for k in (1, 2, 3)]
        self.ypeer, self.xpeer, self.cpeer = self.dev(z, 1 - y, x, c), self.dev(z, y, 1 - x, c), self.dev(z, y, x, 1 - c)
        self.moved = {k: {} for k in ("z", "y", "x1", "x2", "c1", "c2")}
        self.step = 0
        self.local = local

    @staticmethod
    def dev(z, y, x, c):
        return {"clip": z * 2 + y, "frame": x * 2 + c}

    def peers(self):
        return self.zpeers + [self.ypeer, self.xpeer, self.cpeer]

    def span(self, g, first, count):
        _, _, _, r0, rows, unit, c0, width = self.groups[g]
        if unit:
            return pl.multiple_of(r0 + unit * first, 16), unit * count, c0, width
        return r0, rows, pl.multiple_of(512 * first, 512), 512 * count

    def src(self, g, span):
        key, name, lead = self.groups[g][:3]
        r = self.srcs[name] if lead is None else self.srcs[name].at[lead]
        return r.at[pl.ds(span[0], span[1]), pl.ds(span[2], span[3])]

    def dst(self, g, z, y, span):
        key, name, lead = self.groups[g][:3]
        cs = pl.ds(span[2], span[3])
        if name == "table":
            return self.dsts[name].at[z // 2, pl.ds(pl.multiple_of(((z % 2) * 2 + y) * 128 + span[0], 16), span[1]), cs]
        r = self.dsts[name] if lead is None else self.dsts[name].at[lead]
        per = 384 if name == "o" else 96
        return r.at[pl.ds(pl.multiple_of((z * 2 + y) * per + span[0], 16), span[1]), cs]

    def remote(self, kind, i, s, d, peer):
        return pltpu.make_async_remote_copy(
            src_ref=s,
            dst_ref=d,
            send_sem=self.sems[0].at[kind + i],
            recv_sem=self.sems[1].at[kind + i],
            device_id=peer,
            device_id_type=MESH,
        )

    def relay(self, g, kind, items, span, peer):
        return Many(
            [self.remote(22 * g + kind, i, self.dst(g, zz, yy, span), self.dst(g, zz, yy, span), peer) for i, (zz, yy) in items]
        )

    def start_z(self, g):
        two = self.span(g, 3 * self.c + self.x, 2)
        self.moved["z"][g] = Many(
            [self.remote(22 * g, k, self.src(g, two), self.dst(g, self.z, self.y, two), p) for k, p in enumerate(self.zpeers)]
        )

    def begin(self):
        for g in range(self.ahead):
            self.start_z(g)

    def others(self, first):
        return [(q, lax.rem(self.z + q, 4)) for q in range(first, 4)]

    def tick(self):
        s, lag, ng, m, y = self.step, self.lag, len(self.groups), self.moved, self.y
        if s >= ng + 3 * lag:
            return False
        self.step += 1
        if s == 0:
            for cp in self.local:
                cp.wait()
        two, one, half = (3 * self.c + self.x, 2), (3 * self.c + 2 * self.x, 1), (3 * self.c, 3)
        if s < ng:
            m["z"][s].wait_recv()
            if s + self.ahead < ng:
                self.start_z(s + self.ahead)
            m["y"][s] = self.relay(s, 3, [(q, (zz, y)) for q, zz in self.others(0)], self.span(s, *two), self.ypeer)
            m["x1"][s] = self.relay(s, 7, [(q - 1, (zz, y)) for q, zz in self.others(1)], self.span(s, *one), self.xpeer)
        g = s - lag
        if 0 <= g < ng:
            m["y"][g].wait_recv()
            m["x2"][g] = self.relay(g, 10, [(q, (zz, 1 - y)) for q, zz in self.others(0)], self.span(g, *one), self.xpeer)
            m["x1"][g].wait_recv()
            m["c1"][g] = self.relay(g, 14, [(q - 1, (zz, y)) for q, zz in self.others(1)], self.span(g, *half), self.cpeer)
        g = s - 2 * lag
        if 0 <= g < ng:
            m["x2"][g].wait_recv()
            m["c2"][g] = self.relay(g, 17, [(q, (zz, 1 - y)) for q, zz in self.others(0)], self.span(g, *half), self.cpeer)
        g = s - 3 * lag
        if 0 <= g < ng:
            m["c1"][g].wait_recv()
            m["c2"][g].wait_recv()
        return True

    def need(self, key):
        last = max(i for i, g in enumerate(self.groups) if g[0] == key)
        while self.step <= last + 3 * self.lag:
            self.tick()

    def sent(self, key):
        for g, group in enumerate(self.groups):
            for kind in self.moved.values():
                if g in kind and group[0] in (key or group[0]):
                    kind.pop(g).wait_send()

    def finish(self):
        while self.tick():
            pass
        self.sent(None)


PIECES = [(i, 1) for i in range(6)] + [(6, 4), (10, 3), (13, 3)] + [(16 + i, 1) for i in range(4)] + [(20, 4)]


def piece_slots():
    for first, count in PIECES:
        for i in range(8 * count):
            yield first + i // 8, i % 8, i // count, first + i % count


def placement():
    row, col = iota((1024, D), 0), iota((1024, D), 1)
    slot, lane = row >> 7, row & 127
    return jnp.where((col == slot * 96 + lane) & (lane < 96), 1.0, 0.0).astype(bf16)


def layer_kernel(
    gathers, idx, x_ref, g_ref, hq, hp, hi, ho, had, hnm,
    out, ig, gd, spill,
    wq, wp, wi, wo, ad, nm, nbuf, snd, rcv_a, rcv_b, big, x1, x2, tmp, o2, qkv2, a0, a1, us,
    wsem, ssem, rsem, psem, gssem, grsem, nsem,
):
    buf_g, buf_d = big.at[0], big.at[1]
    clip = lax.axis_index("clip")
    me = lax.axis_index("frame")
    nf = 4
    peers = [lax.rem(me + k, nf) for k in range(1, nf)]

    fetch = [pltpu.make_async_copy(s, d, wsem.at[9 + i]) for i, (s, d) in enumerate(((x_ref, ig), (g_ref, out)))]
    for cp in fetch:
        cp.start()
    barrier = pltpu.get_barrier_semaphore()
    groups_of = [{"clip": clip, "frame": d} for d in peers]
    loads = {}
    if gathers:
        own = pl.ds(pl.multiple_of(clip * 96, 16), 96)
        local = [
            (hq.at[0], wq.at[0, own]), (hq.at[1], wq.at[1, own]), (hp.at[0], wp.at[0, own]), (hp.at[1], wp.at[1, own]),
            (hp.at[2], wp.at[2, own]), (hi, wi.at[own]), (ho, wo.at[pl.ds(pl.multiple_of(clip * 384, 16), 384)]),
            (had, big.at[clip // 4, pl.ds(pl.multiple_of((clip % 4) * 128, 16), 128)]),
            (hnm, nbuf.at[pl.ds(pl.multiple_of(clip * 16, 16), 16)]),
        ]
        local = [pltpu.make_async_copy(s, d, wsem.at[i]) for i, (s, d) in enumerate(local)]
        for cp in local:
            cp.start()
        net = Gather(
            {"q": hq, "p": hp, "i": hi, "o": ho, "table": had},
            {"q": wq, "p": wp, "i": wi, "o": wo, "table": big},
            (gssem, grsem),
            local,
        )
        owners = [{"clip": lax.rem(clip + k, 8), "frame": me} for k in range(1, 8)]
        greet = groups_of + owners
    else:
        net = None
        for key, src, dst in (
            ("q0", hq.at[0], wq.at[0]), ("p0", hp.at[0], wp.at[0]), ("p1", hp.at[1], wp.at[1]), ("q1", hq.at[1], wq.at[1]),
            ("p2", hp.at[2], wp.at[2]), ("o", ho, wo), ("i", hi, wi), ("ad", had, ad), ("nm", hnm, nm),
        ):
            loads[key] = pltpu.make_async_copy(src, dst, wsem.at[len(loads)])
            loads[key].start()
        greet = groups_of
    for p in greet:
        pl.semaphore_signal(barrier, inc=1, device_id=p, device_id_type=MESH)
    pl.semaphore_wait(barrier, len(greet))

    def need(key):
        if net is None:
            loads[key].wait()
        else:
            net.need(key)

    def tick():
        if net is not None:
            net.tick()

    if gathers:
        net.begin()
        mine = pl.ds(pl.multiple_of(clip * 16, 16), 16)
        norms = [
            pltpu.make_async_remote_copy(
                src_ref=hnm, dst_ref=nbuf.at[mine], send_sem=nsem.at[0, k], recv_sem=nsem.at[1, k], device_id=p, device_id_type=MESH
            )
            for k, p in enumerate(owners)
        ]
        for cp in norms:
            cp.start()

    def exchange(step, src, index, rcv):
        sent = []
        for k, d in enumerate(peers):
            slot = pl.ds(k * GR, GR)
            snd[slot, :] = dg(onehot(index(d), R), src.get(), 1, 0).astype(bf16)
            cp = pltpu.make_async_remote_copy(
                src_ref=snd.at[slot],
                dst_ref=rcv.at[pl.ds(pl.multiple_of(me * GR, 16), GR)],
                send_sem=ssem.at[step, k],
                recv_sem=rsem.at[step, k],
                device_id={"clip": clip, "frame": d},
                device_id_type=MESH,
            )
            cp.start()
            sent.append(cp)
        rcv[pl.ds(pl.multiple_of(me * GR, 16), GR), :] = dg(onehot(index(me), R), src.get(), 1, 0).astype(bf16)

        def finish():
            for cp in sent:
                cp.wait_recv()
            for cp in sent:
                cp.wait_send()

        return finish

    def gain(k):
        return nm[k : k + 1, :]

    def norm(k, read, put):
        def body(rows):
            hat, _ = norm_rows(read(rows))
            put(rows, (hat * gain(k) + gain(3 + k)).astype(bf16))

        chunks(64, body)

    def rank(h, at, mask, m):
        us[m] = jnp.where(mask, dg(h.get(), ad[:, pl.ds(at, h.width)], 1, 1), 0.0).astype(bf16)

    def forward(m, h, w, width, tile, mask, emit, between=None):
        rank(h, DOWN[m], mask, m)

        def body(c):
            acc = dg(h.get(), w[:, cols(c, tile)], 1, 0)
            acc = acc + dg(us[m], ad[:, cols(UP[m] + c, tile)], 1, 0)
            emit(c, acc)

        tiles(width, tile, body, between)

    def backward(m, dz, w, width, tile, mask, emit, between=None):
        du = jnp.where(mask, dg(dz.get(), ad[:, pl.ds(UP[m], dz.width)], 1, 1), 0.0).astype(bf16)
        us[7] = du

        def body(c):
            acc = dg(dz.get(), w[cols(c, tile), :], 1, 1)
            acc = acc + dg(us[7], ad[:, cols(DOWN[m] + c, tile)], 1, 0)
            emit(c, acc)

        tiles(width, tile, body, between)

    def adapter_grads(m, h, dz):
        gd[:, pl.ds(DOWN[m], h.width)] = dg(us[7], h.get(), 0, 0).astype(gd.dtype)
        gd[:, pl.ds(UP[m], dz.width)] = dg(us[m], dz.get(), 0, 0).astype(gd.dtype)

    p_a0, p_a1 = Part(a0, 0, D), Part(a1, 0, D)
    qkv1, h1 = Part(buf_g, 0, QKV), Part(buf_g, QKV, D)
    xt, o1, m1, spare = (Part(buf_d, D * i, D) for i in range(4))
    p_o2, p_qkv2, p_g, p_d = Part(o2, 0, D), Part(qkv2, 0, QKV), Part(buf_g, 0, FF), Part(buf_d, 0, FF)

    for i, (src, dst) in enumerate(((ig, a0), (out, a1))):
        fetch[i].wait()
        for g in range(4):
            dst[pl.ds(GR * g + 192, 16), :] = jnp.zeros((16, D), bf16)
            dst[pl.ds(GR * g, NP), :] = src[g // 2, g % 2]
        if dst is a0:
            arrive = exchange(0, p_a0, to_message, rcv_a)

    mask_t = clip_mask(392)
    mask_s = clip_mask(416)
    if gathers:
        tick()
        net.need("ad")
        net.sent(["ad"])
        wanted = iota((32, 1), 0)
        wanted = jnp.where(wanted < RANK, idx[0] * RANK + wanted, idx[1] * RANK + wanted - RANK)
        pick = onehot(wanted, 128)
        for owner in range(8):
            rows = pl.ds((owner % 4) * 128, 128)
            part = dg(pick, big[owner // 4, rows, :], 1, 0).astype(bf16)
            for block, slot, of, piece in piece_slots():
                if of == owner:
                    qkv2[pl.ds(block * 32, 32), pl.ds(slot * 128, 128)] = part[:, piece * 128 : piece * 128 + 128]
        place = placement()
        joined = dg(qkv2[pl.ds(0, 768), pl.ds(0, 1024)], place, 1, 0).astype(bf16)
        for block in range(24):
            ad[:, pl.ds(block * D, D)] = joined[block * 32 : block * 32 + 32]
        for cp in norms:
            cp.wait_recv()
        for j in range(8):
            qkv2[pl.ds(0, 16), pl.ds(j * 128, 128)] = nbuf[pl.ds(16 * j, 16), :]
        nm[...] = dg(qkv2[pl.ds(0, 16), pl.ds(0, 1024)], place, 1, 0)
    else:
        need("ad")
        need("nm")
    arrive()
    for i in range(4):
        xt.put(dg(onehot(to_patches(i), R), rcv_a[...], 1, 0).astype(bf16), pl.ds(i * GR, GR))
    norm(0, lambda rows: xt.get(rows).astype(f32), lambda rows, v: h1.put(v, rows))
    need("q0")
    forward(0, h1, wq.at[0], QKV, 768, mask_t, lambda c, acc: qkv1.put(acc.astype(bf16), off=c), tick)
    temporal_loop(lambda rows, n, off, bias: attend_pair(qkv1, rows, n, off, bias, o1), tick)
    need("p0")
    forward(1, o1, wp.at[0], D, 384, mask_t, lambda c, acc: m1.put(acc.astype(bf16), off=c))
    need("p1")
    forward(2, m1, wp.at[1], D, 384, mask_t, lambda c, acc: spare.put(acc.astype(bf16), off=c))
    tick()
    arrive = exchange(1, spare, from_patches, rcv_b)
    tick()
    saves = [pltpu.make_async_copy(b, spill.at[i], psem.at[i]) for i, b in enumerate((buf_g, buf_d))]
    for cp in saves:
        cp.start()
    for cp in saves:
        cp.wait()

    need("o")
    backward(6, p_a1, wo, FF, 768, mask_s, lambda c, acc: p_d.put(acc.astype(bf16), off=c))
    us[8] = us[7]
    arrive()

    for g in range(4):
        rows = pl.ds(g * GR, GR)
        tb = dg(onehot(to_frames(g), R), rcv_b[...], 1, 0)
        x1[rows, :] = a0[rows, :].astype(f32) + tb
    norm(1, lambda rows: x1[rows, :], lambda rows, v: p_o2.put(v, rows))
    need("q1")
    forward(3, p_o2, wq.at[1], QKV, 768, mask_s, lambda c, acc: p_qkv2.put(acc.astype(bf16), off=c), tick)
    spatial_loop(lambda rows, n, off, bias: attend_pair(p_qkv2, rows, n, off, bias, p_o2), tick)
    need("p2")

    def add_spatial(c, acc):
        x2[:, cols(c, 384)] = x1[:, cols(c, 384)] + acc

    forward(4, p_o2, wp.at[2], D, 384, mask_s, add_spatial)

    norm(2, lambda rows: x2[rows, :], lambda rows, v: p_a0.put(v, rows))
    need("i")

    def activate(c, acc):
        tmp_w = acc.shape[1]
        tmp[:, pl.ds(0, tmp_w)] = acc
        @pl.loop(0, R // 32)
        def _(i):
            rows = pl.ds(pl.multiple_of(i * 32, 32), 32)
            v = tmp[rows, pl.ds(0, tmp_w)]
            phi, e = normal_parts(v)
            slope = phi + v * e * 0.3989422804014327
            p_g.put((v * phi).astype(bf16), rows, c)
            p_d.put((p_d.get(rows, c, tmp_w).astype(f32) * slope).astype(bf16), rows, c)

    forward(5, p_a0, wi, FF, 768, mask_s, activate)

    def emit_out(c, acc):
        y = (x2[:, cols(c, 384)] + acc).astype(bf16)
        for g in range(4):
            out[g // 2, g % 2, :, cols(c, 384)] = y[g * GR : g * GR + NP]

    forward(6, p_g, wo, D, 384, mask_s, emit_out)
    us[7] = us[8]
    adapter_grads(6, p_g, p_a1)

    if gathers:
        net.finish()
        for cp in norms:
            cp.wait_send()

    def emit_tmp(c, acc):
        tmp[:, cols(c, 384)] = acc

    backward(5, p_d, wi, D, 384, mask_s, emit_tmp)
    adapter_grads(5, p_a0, p_d)
    loads_back = [pltpu.make_async_copy(spill.at[i], b, psem.at[i]) for i, b in enumerate((buf_g, buf_d))]
    for cp in loads_back:
        cp.start()

    def step_two(rows):
        dx = a1[rows, :].astype(f32) + norm_back_rows(x2[rows, :], gain(2), tmp[rows, :])
        x2[rows, :] = dx
        a0[rows, :] = dx.astype(bf16)

    chunks(64, step_two)

    backward(4, p_a0, wp.at[2], D, 384, mask_s, lambda c, acc: p_a1.put(acc.astype(bf16), off=c))
    adapter_grads(4, p_o2, p_a0)
    spatial_loop(lambda rows, n, off, bias: attend_pair_back(p_qkv2, rows, n, off, bias, p_a1))
    backward(3, p_qkv2, wq.at[1], D, 384, mask_s, emit_tmp)

    def step_one(rows):
        dx = x2[rows, :] + norm_back_rows(x1[rows, :], gain(1), tmp[rows, :])
        x2[rows, :] = dx
        a0[rows, :] = dx.astype(bf16)

    chunks(64, step_one)
    arrive = exchange(2, p_a0, to_message, rcv_a)
    norm(1, lambda rows: x1[rows, :], lambda rows, v: p_a1.put(v, rows))
    adapter_grads(3, p_a1, p_qkv2)
    for cp in loads_back:
        cp.wait()
    arrive()

    for i in range(4):
        p_a0.put(dg(onehot(to_patches(i), R), rcv_a[...], 1, 0).astype(bf16), pl.ds(i * GR, GR))
    backward(2, p_a0, wp.at[1], D, 384, mask_t, lambda c, acc: p_a1.put(acc.astype(bf16), off=c))
    adapter_grads(2, m1, p_a0)
    backward(1, p_a1, wp.at[0], D, 384, mask_t, lambda c, acc: spare.put(acc.astype(bf16), off=c))
    adapter_grads(1, o1, p_a1)
    temporal_loop(lambda rows, n, off, bias: attend_pair_back(qkv1, rows, n, off, bias, spare))
    backward(0, qkv1, wq.at[0], D, 384, mask_t, emit_tmp)

    def step_zero(rows):
        dx = norm_back_rows(xt.get(rows).astype(f32), gain(0), tmp[rows, :])
        a0[rows, :] = dx.astype(bf16)

    chunks(64, step_zero)
    arrive = exchange(3, p_a0, from_patches, rcv_b)
    adapter_grads(0, h1, qkv1)
    arrive()
    for g in range(4):
        dxt = dg(onehot(to_frames(g), R), rcv_b[...], 1, 0)
        total = x2[pl.ds(g * GR, GR), :] + dxt
        ig[g // 2, g % 2] = total.astype(bf16)[:NP]


def layer(gathers, idx, x, g, hq, hp, hi, ho, ad, nm):
    vm = pl.BlockSpec(memory_space=pltpu.VMEM)
    hbm = pl.BlockSpec(memory_space=pl.ANY)
    dma = pltpu.SemaphoreType.DMA
    rows = lambda w, t=bf16: pltpu.VMEM((R, w), t)
    ng = len(gather_groups()) if gathers else 1
    return pl.pallas_call(
        functools.partial(layer_kernel, gathers),
        out_shape=[
            jax.ShapeDtypeStruct(x.shape, bf16),
            jax.ShapeDtypeStruct(x.shape, bf16),
            jax.ShapeDtypeStruct((32, ADW), bf16),
            jax.ShapeDtypeStruct((2, R, FF), bf16),
        ],
        in_specs=[pl.BlockSpec(memory_space=pltpu.SMEM)] + [hbm] * 8,
        out_specs=[vm] * 3 + [hbm],
        scratch_shapes=[
            pltpu.VMEM((2, D, QKV), bf16), pltpu.VMEM((3, D, D), bf16), pltpu.VMEM((D, FF), bf16), pltpu.VMEM((FF, D), bf16),
            pltpu.VMEM((32, ADW), bf16), pltpu.VMEM((16, D), f32), pltpu.VMEM((128, 128), bf16),
            pltpu.VMEM((3 * GR, D), bf16), rows(D), rows(D), pltpu.VMEM((2, R, FF), bf16), rows(D, f32), rows(D, f32), rows(D, f32),
            rows(D), rows(QKV), rows(D), rows(D), pltpu.VMEM((9, R, 32), bf16),
            dma((11,)), dma((4, 3)), dma((4, 3)), dma((2,)), dma((22 * ng,)), dma((22 * ng,)), dma((2, 7)),
        ],
        compiler_params=pltpu.CompilerParams(
            collective_id=1, has_side_effects=True, vmem_limit_bytes=64 * 2**20 - 2**17
        ),
        name="layer",
    )(idx, x, g, hq, hp, hi, ho, ad, nm)


def piece_widths(w):
    return [w] * 6 + [4 * w] + [3 * w] * 2 + [w] * 4 + [4 * w]


def pack_adapters(adapt_down, adapt_down_wide, adapt_up_qkv, adapt_up, adapt_up_wide):
    adapters = adapt_down_wide.shape[0]

    def flat(v):
        return v.reshape(adapters, RANK, -1)

    return jnp.concatenate(
        [
            flat(adapt_down.transpose(1, 3, 0, 2)),
            flat(adapt_down_wide.transpose(0, 2, 1)),
            flat(adapt_up_qkv.transpose(1, 2, 0, 3)),
            flat(adapt_up.transpose(1, 2, 0, 3)),
            flat(adapt_up_wide),
        ],
        axis=-1,
    )


def join_pieces(parts, w):
    joined, at = [], 0
    for width in piece_widths(w):
        piece = parts[:, :, at : at + width]
        joined.append(piece.transpose(1, 0, 2).reshape(parts.shape[1], -1))
        at += width
    return jnp.concatenate(joined, axis=-1)


def split_pieces(rows, w, owners):
    parts, at = [], 0
    for width in piece_widths(w):
        piece = rows[:, at : at + width * owners]
        parts.append(piece.reshape(rows.shape[0], owners, width).transpose(1, 0, 2))
        at += width * owners
    return jnp.concatenate(parts, axis=-1)


def per_device(
    inputs,
    out_grad,
    adapter_index,
    norm_gain,
    norm_bias,
    qkv_weight,
    proj_weight,
    mlp_in,
    mlp_out,
    adapt_down,
    adapt_down_wide,
    adapt_up_qkv,
    adapt_up,
    adapt_up_wide,
):
    owners = lax.axis_size("clip")
    adapters = adapt_down_wide.shape[0]
    clips = inputs.shape[0]
    w = norm_gain.shape[1]
    packed = pack_adapters(adapt_down, adapt_down_wide, adapt_up_qkv, adapt_up, adapt_up_wide)
    norms = jnp.concatenate([norm_gain, norm_bias], axis=0)
    if owners == 8:
        pieces = packed.reshape(adapters * RANK, 24, w)
        table = jnp.pad(pieces, ((0, 0), (0, 0), (0, 128 - w))).reshape(adapters * RANK, 24 * 128)
        own_norms = jnp.pad(norms, ((0, 10), (0, 128 - w)))
        output, input_grad, grads, _ = layer(
            True, adapter_index, inputs, out_grad, qkv_weight, proj_weight, mlp_in, mlp_out, table, own_norms
        )
    else:
        full_qkv = lax.all_gather(qkv_weight, "clip", axis=1, tiled=True)
        full_proj = lax.all_gather(proj_weight, "clip", axis=1, tiled=True)
        full_in = lax.all_gather(mlp_in, "clip", axis=0, tiled=True)
        full_out = lax.all_gather(mlp_out, "clip", axis=0, tiled=True)
        table = lax.all_gather(packed, "clip", axis=0)
        all_norms = lax.all_gather(norms, "clip", axis=0)
        nm = jnp.pad(all_norms.transpose(1, 0, 2).reshape(6, D).astype(f32), ((0, 10), (0, 0)))
        chosen = jnp.take(table, adapter_index, axis=1).reshape(owners, clips * RANK, 24 * w)
        ad = join_pieces(chosen, w)
        output, input_grad, grads, _ = layer(
            False, adapter_index, inputs, out_grad, full_qkv, full_proj, full_in, full_out, ad, nm
        )
    parts = split_pieces(grads, w, owners)
    parts = lax.all_to_all(parts, "clip", split_axis=0, concat_axis=0, tiled=True)
    every = lax.all_gather(adapter_index, "clip", axis=0, tiled=True)
    pick = (every[:, None] == jnp.arange(adapters, dtype=jnp.int32)[None, :]).astype(bf16)
    summed = jnp.einsum(
        "ca,crm->arm", pick, parts.reshape(owners * clips, RANK, 24 * w), preferred_element_type=f32
    )
    summed = lax.psum(summed.astype(bf16), "frame").astype(f32)
    return (output, input_grad) + unpack_grads(summed, w)


def unpack_grads(summed, w):
    adapters = summed.shape[0]
    down = summed[:, :, : 6 * w].reshape(adapters, RANK, 6, w).transpose(2, 0, 3, 1)
    down_wide = summed[:, :, 6 * w : 10 * w].transpose(0, 2, 1)
    up_qkv = summed[:, :, 10 * w : 16 * w].reshape(adapters, RANK, 2, 3 * w).transpose(2, 0, 1, 3)
    up = summed[:, :, 16 * w : 20 * w].reshape(adapters, RANK, 4, w).transpose(2, 0, 1, 3)
    return (down, down_wide, up_qkv, up, summed[:, :, 20 * w :])


def solution(mesh):
    return jax.shard_map(
        per_device,
        mesh=mesh,
        in_specs=(
            P("clip", "frame", None, None),
            P("clip", "frame", None, None),
            P("clip"),
            P(None, "clip"),
            P(None, "clip"),
            P(None, "clip", None),
            P(None, "clip", None),
            P("clip", None),
            P("clip", None),
            P(None, None, "clip", None),
            P(None, "clip", None),
            P(None, None, None, "clip"),
            P(None, None, None, "clip"),
            P(None, None, "clip"),
        ),
        out_specs=(
            P("clip", "frame", None, None),
            P("clip", "frame", None, None),
            P(None, None, "clip", None),
            P(None, "clip", None),
            P(None, None, None, "clip"),
            P(None, None, None, "clip"),
            P(None, None, "clip"),
        ),
        check_vma=False,
    )
```

time: 542 us -> 459 us (0.85)
  Pallas kernels: 392 us -> 339 us
  local copies, waits for them, and re-layouts: 55.8 us -> 28.4 us
    pallas_call x2 -> x1, Pallas kernels: 392 us -> 339 us  [layer(): pl.pallas_call(functools.partial(layer_kernel, gathers), out_shape=[jax.S...]
    reshape x16 -> x1, local copies, waits for them, and re-layouts: 11.3 us -> 1.19 us  [per_device(): pieces = packed.reshape(adapters * RANK, 24, w)]
    unnamed x57 -> x35, local copies, waits for them, and re-layouts: 18.5 us -> 11.5 us
    slice x2 -> x0, local copies, waits for them, and re-layouts: 5.59 us -> none  [the longest x1 4.87 us: per_device(): table = table[:, :, :-128].reshape(owners, adapters, RANK, 24 * w)]
where the time goes in v2:
time: 459 us; the launch traced here: 451 us
  Pallas kernels  339 us (74%)
  blocking collectives  29.2 us (6%)
  local copies, waits for them, and re-layouts  28.4 us (6%)
  waiting for transfers between devices  27.9 us (6%)
  between operations  15.6 us (3%)
  starting transfers between devices  9.02 us (2%)
    pallas_call x1, Pallas kernels, layer(): pl.pallas_call(functools.partial(layer_kernel, gathers), out_shape=[jax.S...  339 us
    unnamed x1, blocking collectives  29.2 us
    psum x1, waiting for transfers between devices, per_device(): summed = lax.psum(summed.astype(bf16), 'frame').astype(f32)  27.9 us
    unnamed x35, local copies, waits for them, and re-layouts  11.5 us
  transfers between devices with their start and end apart: 2, of which 1 were waited for; matrix products, arithmetic and copies ran while one was open for 1% of the time, Pallas kernels for 0%

profile of v2, /device:TPU:0, one launch (start us, length us, event | category | flops | bytes accessed | tf_op | source)
XLA Modules:
  0.0 451.1 jit_solution(1962776690299186432)
XLA Ops:
  7.2 0.0 copy-start.5
  7.2 0.0 copy-start.6
  7.2 0.0 copy-start.7
  7.2 1.1 copy.30
  8.3 0.2 reshape.84
  8.5 1.1 copy.31
  9.6 0.2 reshape.85
  9.8 0.0 copy-done.5
  9.8 0.1 copy.32
  9.9 0.1 reshape.86
  10.1 0.0 copy-done.6
  10.1 0.4 concatenate.9
  10.5 1.2 reshape.87
  11.7 0.2 pad.8
  11.8 0.0 copy-start.3
  11.9 1.0 copy.80
  12.9 0.5 copy-done.3
  13.4 1.2 copy.33.x_ref
  14.6 0.6 copy-done.4
  15.1 1.2 copy.34.g_ref
  16.3 0.0 copy-done.8
  16.3 0.6 fusion.6.hnm
  16.9 338.9 %layer.1 = (bf16[2,2,196,768]{3,2,1,0:T(8,128)(2,1)}, bf16[2,2,196,768]{3,2,1,0:T(8,128)(2,1)}, bf16[32,18432]{1,0:T(8,128)(2,1)}, bf16[2,832,3072]{2,1,0:T(8,128)(2,1)}) custom-call(s32[2]{0:T(128)} %idx.1, bf16[2,2,196,768]{3,2,1,0:T(8,128)(2,1)} %copy.33.x_ref, bf16[2,2,196,768]{3,2,1,0:T(8,128)(2,1)} %copy.34.g_ref, bf16[2,96,2304]{2,1,0:T(8,128)(2,1)} %hq.1, ...), custom_call_target="tpu_custom_call" | custom-call | tf_op jit(solution)/shard_map/layer/pallas_call | solution.py:680
  355.8 1.1 fusion.11
  356.9 1.0 fusion.12
  357.9 1.1 fusion.10
  359.0 0.1 reshape.100
  359.1 0.1 reshape.101
  359.2 0.1 reshape.98
  359.3 0.1 reshape.99
  359.5 0.1 reshape.93
  359.6 0.1 reshape.94
  359.7 0.1 reshape.91
  359.8 0.1 reshape.92
  360.0 0.1 reshape.89
  360.1 0.1 reshape.90
  360.2 0.3 reshape.96
  360.5 0.3 reshape.97
  361.1 3.5 concatenate.11
  364.6 9.0 %all-to-all-start = ((bf16[8,32,2304]{2,1,0:T(8,128)(2,1)}), bf16[8,32,2304]{2,1,0:T(8,128)(2,1)S(1)}, u32[]{:S(2)}, u32[]{:S(2)}) async-start(bf16[8,32,2304]{2,1,0:T(8,128)(2,1)} %concatenate.11), calls=%async_computation | async-start | bytes 2359296 | tf_op jit(solution)/shard_map/all_to_all | solution.py:787
  373.6 0.0 all-reduce.5.cloned.1.call-start
  373.7 0.6 dynamic-slice
  374.9 0.2 dynamic-update-slice
  375.2 29.2 %all-reduce.2 = s32[16]{0:T(128)S(1)} all-reduce(s32[16]{0:T(128)S(1)} %dynamic-update-slice), channel_id=1, replica_groups=mesh['clip'=8,'frame'=4] {'clip'}, use_global_device_ids=true, to_apply=%add.2 | all-reduce | flops 16 | bytes 128
  404.4 0.0 all-to-all-done
  404.4 1.3 convolution_convert_fusion
  405.8 0.0 all-reduce.5.cloned.1.call-update
  405.8 0.0 copy-done.2
  405.8 0.0 copy-start.1
  405.8 1.9 copy.53
  407.8 1.9 copy.54
  409.7 27.9 %all-reduce.5.cloned.1.call-done = bf16[8,16,2304]{2,0,1:T(8,128)(2,1)} async-done(((bf16[8,16,2304]{2,0,1:T(8,128)(2,1)}), bf16[8,16,2304]{2,0,1:T(8,128)(2,1)}) %all-reduce.5.cloned.1.call-update) | async-done | bytes 589840 | tf_op jit(solution)/shard_map/psum | solution.py:793
  437.6 1.1 fusion.14
  438.8 0.1 copy.50
  438.8 0.2 reshape.104
  439.0 0.8 copy.55
  439.8 0.1 convert_element_type.12
  439.9 0.1 slice_bitcast_fusion
  440.0 0.7 copy.56
  440.8 0.3 reshape.105
  441.1 0.9 copy.81
  442.0 0.2 reshape.106
  442.1 0.9 copy.82
  443.0 0.7 copy.57
  (22 shorter events, 0.2 us)
Async XLA Ops:
  7.2 2.6 copy-start.5
  7.2 2.9 copy-start.6
  7.2 2.9 copy-start.7
  11.8 1.6 copy-start.3
  13.4 1.7 copy-start.4
  15.1 1.2 copy-start.8
  15.1 1.2 copy-start.9
  364.6 9.0 %copy-start.11 = (u32[32]{0:T(128)S(1)}, u32[32]{0:T(128)}, u32[]{:S(2)}) copy-start(u32[32]{0:T(128)} %constant.12) | copy-start | bytes 388
  364.6 10.3 %copy-start.10 = (s32[2]{0:T(128)S(1)}, s32[2]{0:T(128)}, u32[]{:S(2)}) copy-start(s32[2]{0:T(128)} %idx.1) | copy-start | bytes 28
  364.6 39.8 %all-to-all-start = ((bf16[8,32,2304]{2,1,0:T(8,128)(2,1)}), bf16[8,32,2304]{2,1,0:T(8,128)(2,1)S(1)}, u32[]{:S(2)}, u32[]{:S(2)}) async-start(bf16[8,32,2304]{2,1,0:T(8,128)(2,1)} %concatenate.11), calls=%async_computation | async-start | bytes 2359296 | tf_op jit(solution)/shard_map/all_to_all | solution.py:787
  373.6 64.0 %all-reduce.5.cloned.1.call-start = ((), (), s32[]{:S(2)}) async-start(), calls=%async_computation.1 | async-start | bytes 1179648 | tf_op jit(solution)/shard_map/psum | solution.py:793
  404.4 1.4 copy-start.2
  405.8 2.0 copy-start.1
  438.7 1.1 copy-start
Sparse Core Ops, SparseCore 0:
  405.9 31.6 all-reduce.4

commit v3 on v2

--- a/solution.py
+++ b/solution.py
@@ -109,9 +109,8 @@
 
     else:
         for c in range(0, total, tile):
+            between(c)
             body(c)
-            if c + tile < total:
-                between()
 
 
 def norm_rows(v):
@@ -129,85 +128,67 @@
     return rstd * (g - m1 - hat * m2)
 
 
-def head_masks(n):
-    first = iota((n, 128), 1) < 64
-    one, zero = jnp.ones((n, 128), bf16), jnp.zeros((n, 128), bf16)
-    return jnp.where(first, one, zero), jnp.where(first, zero, one)
-
-
-def eye(n):
-    return jnp.where(iota((n, n), 0) == iota((n, n), 1), 1.0, 0.0).astype(bf16)
-
-
-def attend_pair(qkv, rows, n, off, bias, out):
-    q = qkv.get(rows, off, 128)
-    k = qkv.get(rows, D + off, 128)
-    v_t = dg(eye(128), qkv.get(rows, 2 * D + off, 128), 1, 1).astype(bf16)
-    parts = []
-    for h, hm in enumerate(head_masks(n)):
-        s = dg(k * (hm * 0.125).astype(bf16), q, 1, 1) + bias
-        p = jnp.exp(s - jnp.max(s, axis=0, keepdims=True))
-        total = jnp.sum(p, axis=0, keepdims=True)
-        parts.append(dg(v_t[64 * h : 64 * h + 64], p.astype(bf16), 1, 0) * (1.0 / total))
-    o_t = jnp.concatenate(parts, axis=0).astype(bf16)
-    out.put(dg(eye(n), o_t, 1, 1).astype(bf16), rows, off)
-
-
-def attend_pair_back(qkv, rows, n, off, bias, dout):
-    q = qkv.get(rows, off, 128)
-    k = qkv.get(rows, D + off, 128)
-    v = qkv.get(rows, 2 * D + off, 128)
-    do = dout.get(rows, off, 128)
-    k_t = (dg(eye(128), k, 1, 1) * 0.125).astype(bf16)
-    dq_t, dks, dvs = [], [], []
-    for h, hm in enumerate(head_masks(n)):
-        s = dg(k * (hm * 0.125).astype(bf16), q, 1, 1) + bias
-        p = jnp.exp(s - jnp.max(s, axis=0, keepdims=True))
-        p = p * (1.0 / jnp.sum(p, axis=0, keepdims=True))
-        dp = dg(v * hm, do, 1, 1)
-        dvs.append(dg(p.astype(bf16), do, 1, 0))
-        ds = (p * (dp - jnp.sum(dp * p, axis=0, keepdims=True))).astype(bf16)
-        dq_t.append(dg(k_t[64 * h : 64 * h + 64], ds, 1, 0))
-        dks.append(dg(ds, q, 1, 0))
-    first = iota((n, 128), 1) < 64
-    dq = dg(eye(n), jnp.concatenate(dq_t, axis=0).astype(bf16), 1, 1)
-    qkv.put(dq.astype(bf16), rows, off)
-    qkv.put((jnp.where(first, dks[0], dks[1]) * 0.125).astype(bf16), rows, D + off)
-    qkv.put(jnp.where(first, dvs[0], dvs[1]).astype(bf16), rows, 2 * D + off)
-
-
-def spatial_loop(body, between=None):
-    bias = jnp.where(iota((GR, 1), 0) < NP, 0.0, -BIG)
-
-    def group(g):
-        @pl.loop(0, 6)
-        def _(i):
-            body(pl.ds(g * GR if isinstance(g, int) else pl.multiple_of(g * GR, 16), GR), GR, i * 128, bias)
-
-    if between is None:
-        pl.loop(0, 4)(group)
+def split_heads(v):
+    first = iota(v.shape, 1) < 64
+    zero = jnp.zeros(v.shape, bf16)
+    return jnp.concatenate([jnp.where(first, v, zero), jnp.where(first, zero, v)], axis=0)
+
+
+def join_heads(v):
+    n = v.shape[0] // 2
+    return jnp.where(iota((n, 128), 1) < 64, v[:n], v[n:])
+
+
+def attend(qkv, rows, n, bias, out, pairs):
+    q = [split_heads(qkv.get(rows, o, 128) * bf16(0.125)) for o in pairs]
+    s = [dg(a, qkv.get(rows, D + o, 128), 1, 1) + bias for a, o in zip(q, pairs)]
+    p = [jnp.exp(a - jnp.max(a, axis=1, keepdims=True)).astype(bf16) for a in s]
+    ones = jnp.ones((n, 128), bf16)
+    for a, o in zip(p, pairs):
+        r = dg(a, jnp.concatenate([qkv.get(rows, 2 * D + o, 128), ones], axis=1), 1, 0)
+        out.put(join_heads(r[:, :128] / r[:, 128:]).astype(bf16), rows, o)
+
+
+def attend_back(qkv, rows, n, bias, dout, pairs, sums_by_product):
+    q = [split_heads(qkv.get(rows, o, 128) * bf16(0.125)) for o in pairs]
+    k = [qkv.get(rows, D + o, 128) for o in pairs]
+    g = [split_heads(dout.get(rows, o, 128)) for o in pairs]
+    s = [dg(a, b, 1, 1) + bias for a, b in zip(q, k)]
+    dp = [dg(a, qkv.get(rows, 2 * D + o, 128), 1, 1) for a, o in zip(g, pairs)]
+    p = [jnp.exp(a - jnp.max(a, axis=1, keepdims=True)) for a in s]
+    if sums_by_product:
+        ones = jnp.ones((n, n), bf16)
+        p = [a * (1.0 / dg(a.astype(bf16), ones, 1, 0)) for a in p]
     else:
-        for g in range(4):
-            group(g)
-            between()
-
-
-def temporal_loop(body, between=None):
+        p = [a * (1.0 / jnp.sum(a, axis=1, keepdims=True)) for a in p]
+    ds = [(a * (b - jnp.sum(a * b, axis=1, keepdims=True))).astype(bf16) for a, b in zip(p, dp)]
+    for i, o in enumerate(pairs):
+        qkv.put((join_heads(dg(ds[i], k[i], 1, 0)) * 0.125).astype(bf16), rows, o)
+        qkv.put(dg(ds[i], q[i], 0, 0).astype(bf16), rows, D + o)
+        qkv.put(dg(p[i].astype(bf16), g[i], 0, 0).astype(bf16), rows, 2 * D + o)
+
+
+def spatial_loop(count, body):
+    bias = jnp.where(iota((1, GR), 1) < NP, 0.0, -BIG)
+    steps = 6 // count
+
+    @pl.loop(0, 4 * steps)
+    def _(i):
+        pairs = [((i % steps) * count + k) * 128 for k in range(count)]
+        body(pl.ds(pl.multiple_of((i // steps) * GR, 16), GR), GR, bias, pairs)
+
+
+def temporal_loop(body):
+    pairs = range(0, D, 128)
+
     def bias(n):
-        return jnp.where((iota((n, n), 0) >> 3) == (iota((n, n), 1) >> 3), 0.0, -BIG)
-
-    def block(i, n):
-        rows = pl.ds(i * 128 if isinstance(i, int) else pl.multiple_of(i * 128, 128), n)
-        for u in range(6):
-            body(rows, n, u * 128, bias(n))
-
-    if between is None:
-        pl.loop(0, 6)(lambda i: block(i, 128))
-    else:
-        for k in range(3):
-            pl.loop(2 * k, 2 * k + 2)(lambda i: block(i, 128))
-            between()
-    block(6, 64)
+        return jnp.where(((iota((2 * n, n), 0) & (n - 1)) >> 3) == (iota((2 * n, n), 1) >> 3), 0.0, -BIG)
+
+    @pl.loop(0, 6)
+    def _(i):
+        body(pl.ds(pl.multiple_of(i * 128, 128), 128), 128, bias(128), pairs)
+
+    body(pl.ds(768, 64), 64, bias(64), pairs)
 
 
 class Many:
@@ -226,13 +207,12 @@
 
 
 def gather_groups():
-    out = [("ad", "table", None, 32 * k, 32, 0, 0, FF) for k in range(4)]
-    out += [("q0", "q", 0, 0, 96, 16, c, D) for c in range(0, QKV, D)]
+    out = [(f"q0{c}", "q", 0, 0, 96, 16, c, D) for c in range(0, QKV, D)]
     out += [("p0", "p", 0, 0, 96, 16, 0, D), ("p1", "p", 1, 0, 96, 16, 0, D)]
-    out += [("q1", "q", 1, 0, 96, 16, c, D) for c in range(0, QKV, D)]
+    out += [(f"q1{c}", "q", 1, 0, 96, 16, c, D) for c in range(0, QKV, D)]
     out += [("p2", "p", 2, 0, 96, 16, 0, D)]
     out += [("o", "o", None, r, 96, 16, 0, D) for r in range(0, 384, 96)]
-    out += [("i", "i", None, 0, 96, 16, c, D) for c in range(0, FF, D)]
+    out += [(f"i{c}", "i", None, 0, 96, 16, c, D) for c in range(0, FF, D)]
     return out
 
 
@@ -246,7 +226,7 @@
         z, y, x, c = self.z, self.y, self.x, self.c
         self.zpeers = [self.dev(lax.rem(z + k, 4), y, x, c) for k in (1, 2, 3)]
         self.ypeer, self.xpeer, self.cpeer = self.dev(z, 1 - y, x, c), self.dev(z, y, 1 - x, c), self.dev(z, y, x, 1 - c)
-        self.moved = {k: {} for k in ("z", "y", "x1", "x2", "c1", "c2")}
+        self.moved = {k: {} for k in ("z", "y0", "y", "x1", "x2", "c1", "c2")}
         self.step = 0
         self.local = local
 
@@ -259,9 +239,7 @@
 
     def span(self, g, first, count):
         _, _, _, r0, rows, unit, c0, width = self.groups[g]
-        if unit:
-            return pl.multiple_of(r0 + unit * first, 16), unit * count, c0, width
-        return r0, rows, pl.multiple_of(512 * first, 512), 512 * count
+        return pl.multiple_of(r0 + unit * first, 16), unit * count, c0, width
 
     def src(self, g, span):
         key, name, lead = self.groups[g][:3]
@@ -271,8 +249,6 @@
     def dst(self, g, z, y, span):
         key, name, lead = self.groups[g][:3]
         cs = pl.ds(span[2], span[3])
-        if name == "table":
-            return self.dsts[name].at[z // 2, pl.ds(pl.multiple_of(((z % 2) * 2 + y) * 128 + span[0], 16), span[1]), cs]
         r = self.dsts[name] if lead is None else self.dsts[name].at[lead]
         per = 384 if name == "o" else 96
         return r.at[pl.ds(pl.multiple_of((z * 2 + y) * per + span[0], 16), span[1]), cs]
@@ -297,6 +273,7 @@
         self.moved["z"][g] = Many(
             [self.remote(22 * g, k, self.src(g, two), self.dst(g, self.z, self.y, two), p) for k, p in enumerate(self.zpeers)]
         )
+        self.moved["y0"][g] = Many([self.remote(22 * g, 3, self.src(g, two), self.dst(g, self.z, self.y, two), self.ypeer)])
 
     def begin(self):
         for g in range(self.ahead):
@@ -318,10 +295,11 @@
             m["z"][s].wait_recv()
             if s + self.ahead < ng:
                 self.start_z(s + self.ahead)
-            m["y"][s] = self.relay(s, 3, [(q, (zz, y)) for q, zz in self.others(0)], self.span(s, *two), self.ypeer)
+            m["y"][s] = self.relay(s, 4, [(q - 1, (zz, y)) for q, zz in self.others(1)], self.span(s, *two), self.ypeer)
             m["x1"][s] = self.relay(s, 7, [(q - 1, (zz, y)) for q, zz in self.others(1)], self.span(s, *one), self.xpeer)
         g = s - lag
         if 0 <= g < ng:
+            m["y0"][g].wait_recv()
             m["y"][g].wait_recv()
             m["x2"][g] = self.relay(g, 10, [(q, (zz, 1 - y)) for q, zz in self.others(0)], self.span(g, *one), self.xpeer)
             m["x1"][g].wait_recv()
@@ -341,16 +319,12 @@
         while self.step <= last + 3 * self.lag:
             self.tick()
 
-    def sent(self, key):
-        for g, group in enumerate(self.groups):
-            for kind in self.moved.values():
-                if g in kind and group[0] in (key or group[0]):
-                    kind.pop(g).wait_send()
-
     def finish(self):
         while self.tick():
             pass
-        self.sent(None)
+        for kind in self.moved.values():
+            for cps in kind.values():
+                cps.wait_send()
 
 
 PIECES = [(i, 1) for i in range(6)] + [(6, 4), (10, 3), (13, 3)] + [(16 + i, 1) for i in range(4)] + [(20, 4)]
@@ -362,25 +336,131 @@
             yield first + i // 8, i % 8, i // count, first + i % count
 
 
-def placement():
-    row, col = iota((1024, D), 0), iota((1024, D), 1)
-    slot, lane = row >> 7, row & 127
-    return jnp.where((col == slot * 96 + lane) & (lane < 96), 1.0, 0.0).astype(bf16)
+def placement(part):
+    row = iota((256, 1), 0)
+    lane = row & 127
+    return onehot(jnp.where(lane < 96, (2 * part + (row >> 7)) * 96 + lane, -1), D)
+
+
+def place(rows):
+    total = dg(rows(0), placement(0), 1, 0)
+    for part in range(1, 4):
+        total = total + dg(rows(part), placement(part), 1, 0)
+    return total
+
+
+def pick_rows(index):
+    return jnp.where(iota((256, 128), 1) == index[...], 1.0, 0.0).astype(bf16)
+
+
+BATCHES = ([3, 4, 5, 6, 7, 8, 9, 13, 14, 15, 18, 19, 20, 21, 22, 23], [0, 1, 2, 10, 11, 12, 16, 17])
+PLACES = {p: i for i, p in enumerate(BATCHES[0] + BATCHES[1])}
+
+
+class Reduce:
+    def __init__(self, batch, gd, work, stage_rows, received, result, nidx, sems):
+        self.batch, self.gd, self.work, self.stage_rows = batch, gd, work, stage_rows
+        self.received, self.result, self.nidx, self.sems = received, result, nidx, sems
+        clip, frame = lax.axis_index("clip"), lax.axis_index("frame")
+        self.clip, self.frame, self.x, self.c = clip, frame, frame // 2, frame % 2
+        self.xpeer = {"clip": clip, "frame": (1 - self.x) * 2 + self.c}
+        self.cpeer = {"clip": clip, "frame": self.x * 2 + 1 - self.c}
+        self.width = len(BATCHES[batch]) * 32
+        self.count = 0
+        self.sent = []
+
+    def lanes(self, quarter):
+        return pl.ds(pl.multiple_of(2048 * self.batch + self.width * quarter, 128), self.width)
+
+    def send(self, src, dst, peer):
+        i = 16 * self.batch + self.count
+        self.count += 1
+        cp = pltpu.make_async_remote_copy(
+            src_ref=src, dst_ref=dst, send_sem=self.sems.at[0, i], recv_sem=self.sems.at[1, i], device_id=peer, device_id_type=MESH
+        )
+        cp.start()
+        self.sent.append(cp)
+        return cp
+
+    def add(self, first_row, quarter):
+        ls = self.lanes(quarter)
+        total = self.work[pl.ds(0, 256), ls].astype(f32) + self.work[pl.ds(first_row, 256), ls].astype(f32)
+        self.work[pl.ds(0, 256), ls] = total.astype(bf16)
+
+    def split(self):
+        pieces = BATCHES[self.batch]
+        for i, block in enumerate(pieces):
+            self.stage_rows[pl.ds(32 * i, 32), :] = self.gd[:, pl.ds(block * D, D)]
+        for part in range(4):
+            rows = self.stage_rows[pl.ds(0, 32 * len(pieces)), :]
+            parts = dg(rows, placement(part), 1, 1).astype(bf16)
+            for block, slot, owner, piece in piece_slots():
+                if block in pieces and slot // 2 == part:
+                    i = pieces.index(block)
+                    tile = parts[32 * i : 32 * i + 32, 128 * (slot % 2) : 128 * (slot % 2) + 128]
+                    self.work[pl.ds(32 * owner, 32), pl.ds(128 * PLACES[piece], 128)] = tile
+        self.core = []
+        for xx in range(2):
+            ls = self.lanes(2 * xx + 1 - self.c)
+            self.core.append(self.send(self.work.at[pl.ds(0, 256), ls], self.work.at[pl.ds(256, 256), ls], self.cpeer))
+
+    def over_x(self):
+        for xx in range(2):
+            self.core[xx].wait_recv()
+        for xx in range(2):
+            self.add(256, 2 * xx + self.c)
+        ls = self.lanes(2 * (1 - self.x) + self.c)
+        self.across = self.send(self.work.at[pl.ds(0, 256), ls], self.work.at[pl.ds(512, 256), ls], self.xpeer)
+
+    def to_owners(self):
+        self.across.wait_recv()
+        self.add(512, self.frame)
+        ls = self.lanes(self.frame)
+        self.here = pl.ds(512 * self.batch, self.width)
+        mine = pl.ds(pl.multiple_of(32 * self.clip, 32), 32)
+        self.received[mine, self.here] = self.work[mine, ls]
+        self.owned = []
+        for k in range(1, 8):
+            j = lax.rem(self.clip + k, 8)
+            rows = pl.ds(pl.multiple_of(32 * j, 32), 32)
+            self.owned.append(
+                self.send(self.work.at[rows, ls], self.received.at[mine, self.here], {"clip": j, "frame": self.frame})
+            )
+
+    def by_adapter(self):
+        for cp in self.owned:
+            cp.wait_recv()
+        ls = self.lanes(self.frame)
+        self.result[:, ls] = dg(pick_rows(self.nidx), self.received[:, self.here], 0, 0).astype(bf16)
+        same = self.result.at[:, ls]
+        self.back = [self.send(same, same, p) for p in (self.xpeer, self.cpeer)]
+
+    def spread(self):
+        self.back[0].wait_recv()
+        same = self.result.at[:, self.lanes(2 * (1 - self.x) + self.c)]
+        self.last = self.send(same, same, self.cpeer)
+
+    def finish(self):
+        self.back[1].wait_recv()
+        self.last.wait_recv()
+        for cp in self.sent:
+            cp.wait_send()
 
 
 def layer_kernel(
-    gathers, idx, x_ref, g_ref, hq, hp, hi, ho, had, hnm,
-    out, ig, gd, spill,
-    wq, wp, wi, wo, ad, nm, nbuf, snd, rcv_a, rcv_b, big, x1, x2, tmp, o2, qkv2, a0, a1, us,
-    wsem, ssem, rsem, psem, gssem, grsem, nsem,
+    gathers, hidx, x_ref, g_ref, hq, hp, hi, ho, had, hnm,
+    out, ig, grads, spill,
+    wq, wp, wi, wo, ad, nm, nbuf, nidx, gd, received, rcv_a, rcv_b, big, x1, x2, tmp, o2, qkv2, a0, a1, us,
+    wsem, ssem, rsem, psem, gssem, grsem, nsem, asem, bsem,
 ):
     buf_g, buf_d = big.at[0], big.at[1]
+
     clip = lax.axis_index("clip")
     me = lax.axis_index("frame")
     nf = 4
     peers = [lax.rem(me + k, nf) for k in range(1, nf)]
 
-    fetch = [pltpu.make_async_copy(s, d, wsem.at[9 + i]) for i, (s, d) in enumerate(((x_ref, ig), (g_ref, out)))]
+    fetch = [pltpu.make_async_copy(s, d, wsem.at[10 + i]) for i, (s, d) in enumerate(((x_ref, ig), (g_ref, out)))]
     for cp in fetch:
         cp.start()
     barrier = pltpu.get_barrier_semaphore()
@@ -391,17 +471,17 @@
         local = [
             (hq.at[0], wq.at[0, own]), (hq.at[1], wq.at[1, own]), (hp.at[0], wp.at[0, own]), (hp.at[1], wp.at[1, own]),
             (hp.at[2], wp.at[2, own]), (hi, wi.at[own]), (ho, wo.at[pl.ds(pl.multiple_of(clip * 384, 16), 384)]),
-            (had, big.at[clip // 4, pl.ds(pl.multiple_of((clip % 4) * 128, 16), 128)]),
-            (hnm, nbuf.at[pl.ds(pl.multiple_of(clip * 16, 16), 16)]),
+            (had, big.at[1, pl.ds(0, 128)]), (hnm, nbuf.at[pl.ds(pl.multiple_of(clip * 16, 16), 16)]),
+            (hidx, nidx.at[pl.ds(pl.multiple_of(clip * 32, 32), 32)]),
         ]
         local = [pltpu.make_async_copy(s, d, wsem.at[i]) for i, (s, d) in enumerate(local)]
         for cp in local:
             cp.start()
         net = Gather(
-            {"q": hq, "p": hp, "i": hi, "o": ho, "table": had},
-            {"q": wq, "p": wp, "i": wi, "o": wo, "table": big},
+            {"q": hq, "p": hp, "i": hi, "o": ho},
+            {"q": wq, "p": wp, "i": wi, "o": wo},
             (gssem, grsem),
-            local,
+            local[:7],
         )
         owners = [{"clip": lax.rem(clip + k, 8), "frame": me} for k in range(1, 8)]
         greet = groups_of + owners
@@ -418,35 +498,46 @@
         pl.semaphore_signal(barrier, inc=1, device_id=p, device_id_type=MESH)
     pl.semaphore_wait(barrier, len(greet))
 
-    def need(key):
-        if net is None:
+    def need(key, c=""):
+        if net is not None:
+            net.need(f"{key}{c}")
+        elif not c:
             loads[key].wait()
-        else:
-            net.need(key)
+
+    def need_tiles(key):
+        def between(c):
+            if c:
+                tick()
+            need(key, c)
+
+        return between
 
     def tick():
         if net is not None:
             net.tick()
 
     if gathers:
+
+        def to(peer, src, dst, sems, i):
+            cp = pltpu.make_async_remote_copy(
+                src_ref=src, dst_ref=dst, send_sem=sems.at[0, i], recv_sem=sems.at[1, i], device_id=peer, device_id_type=MESH
+            )
+            cp.start()
+            return cp
+
+        rows16 = pl.ds(pl.multiple_of(clip * 16, 16), 16)
+        rows32 = pl.ds(pl.multiple_of(clip * 32, 32), 32)
+        small = [to(p, hidx, nidx.at[rows32], nsem, k) for k, p in enumerate(owners)]
+        small += [to(p, hnm, nbuf.at[rows16], nsem, 7 + k) for k, p in enumerate(owners)]
         net.begin()
-        mine = pl.ds(pl.multiple_of(clip * 16, 16), 16)
-        norms = [
-            pltpu.make_async_remote_copy(
-                src_ref=hnm, dst_ref=nbuf.at[mine], send_sem=nsem.at[0, k], recv_sem=nsem.at[1, k], device_id=p, device_id_type=MESH
-            )
-            for k, p in enumerate(owners)
-        ]
-        for cp in norms:
-            cp.start()
 
     def exchange(step, src, index, rcv):
         sent = []
         for k, d in enumerate(peers):
             slot = pl.ds(k * GR, GR)
-            snd[slot, :] = dg(onehot(index(d), R), src.get(), 1, 0).astype(bf16)
+            o2[slot, :] = dg(onehot(index(d), R), src.get(), 1, 0).astype(bf16)
             cp = pltpu.make_async_remote_copy(
-                src_ref=snd.at[slot],
+                src_ref=o2.at[slot],
                 dst_ref=rcv.at[pl.ds(pl.multiple_of(me * GR, 16), GR)],
                 send_sem=ssem.at[step, k],
                 recv_sem=rsem.at[step, k],
@@ -476,32 +567,38 @@
         chunks(64, body)
 
     def rank(h, at, mask, m):
-        us[m] = jnp.where(mask, dg(h.get(), ad[:, pl.ds(at, h.width)], 1, 1), 0.0).astype(bf16)
+        us[:, pl.ds(32 * m, 32)] = jnp.where(mask, dg(h.get(), ad[:, pl.ds(at, h.width)], 1, 1), 0.0).astype(bf16)
 
     def forward(m, h, w, width, tile, mask, emit, between=None):
         rank(h, DOWN[m], mask, m)
 
         def body(c):
             acc = dg(h.get(), w[:, cols(c, tile)], 1, 0)
-            acc = acc + dg(us[m], ad[:, cols(UP[m] + c, tile)], 1, 0)
+            acc = acc + dg(us[:, pl.ds(32 * m, 32)], ad[:, cols(UP[m] + c, tile)], 1, 0)
             emit(c, acc)
 
         tiles(width, tile, body, between)
 
+    def rank_back(m, dz, mask):
+        du = jnp.where(mask, dg(dz.get(), ad[:, pl.ds(UP[m], dz.width)], 1, 1), 0.0).astype(bf16)
+        us[:, pl.ds(224, 32)] = du
+
     def backward(m, dz, w, width, tile, mask, emit, between=None):
-        du = jnp.where(mask, dg(dz.get(), ad[:, pl.ds(UP[m], dz.width)], 1, 1), 0.0).astype(bf16)
-        us[7] = du
+        rank_back(m, dz, mask)
+        backward_rows(m, dz, w, width, tile, emit, between)
+
+    def backward_rows(m, dz, w, width, tile, emit, between=None):
 
         def body(c):
             acc = dg(dz.get(), w[cols(c, tile), :], 1, 1)
-            acc = acc + dg(us[7], ad[:, cols(DOWN[m] + c, tile)], 1, 0)
+            acc = acc + dg(us[:, pl.ds(224, 32)], ad[:, cols(DOWN[m] + c, tile)], 1, 0)
             emit(c, acc)
 
         tiles(width, tile, body, between)
 
     def adapter_grads(m, h, dz):
-        gd[:, pl.ds(DOWN[m], h.width)] = dg(us[7], h.get(), 0, 0).astype(gd.dtype)
-        gd[:, pl.ds(UP[m], dz.width)] = dg(us[m], dz.get(), 0, 0).astype(gd.dtype)
+        gd[:, pl.ds(DOWN[m], h.width)] = dg(us[:, pl.ds(224, 32)], h.get(), 0, 0).astype(gd.dtype)
+        gd[:, pl.ds(UP[m], dz.width)] = dg(us[:, pl.ds(32 * m, 32)], dz.get(), 0, 0).astype(gd.dtype)
 
     p_a0, p_a1 = Part(a0, 0, D), Part(a1, 0, D)
     qkv1, h1 = Part(buf_g, 0, QKV), Part(buf_g, QKV, D)
@@ -519,39 +616,67 @@
     mask_t = clip_mask(392)
     mask_s = clip_mask(416)
     if gathers:
+        for cp in local[7:]:
+            cp.wait()
+        for cp in small[:7]:
+            cp.wait_recv()
+        pick = pick_rows(nidx)
+        quarter = cols(me * D, D)
+        chosen = big.at[1, pl.ds(128, 256), pl.ds(0, D)]
+        big[1, pl.ds(128, 256), pl.ds(0, D)] = dg(pick, big[1, pl.ds(0, 128), quarter], 1, 0).astype(bf16)
+        picked = []
+        for k, p in enumerate(owners):
+            rows = pl.ds(pl.multiple_of(128 + 32 * p["clip"], 32), 32)
+            picked.append(to(p, big.at[1, rows, pl.ds(0, D)], big.at[0, rows32, quarter], asem, k))
+        big[0, rows32, quarter] = big[1, pl.ds(pl.multiple_of(128 + 32 * clip, 32), 32), pl.ds(0, D)]
         tick()
-        net.need("ad")
-        net.sent(["ad"])
-        wanted = iota((32, 1), 0)
-        wanted = jnp.where(wanted < RANK, idx[0] * RANK + wanted, idx[1] * RANK + wanted - RANK)
-        pick = onehot(wanted, 128)
+        for cp in picked:
+            cp.wait_recv()
+
+        def block_of(frame):
+            return big.at[0, pl.ds(0, 256), cols(frame * D, D)]
+
+        x, c = me // 2, me % 2
+        xpeer, cpeer = {"clip": clip, "frame": (1 - x) * 2 + c}, {"clip": clip, "frame": x * 2 + 1 - c}
+        picked.append(to(xpeer, block_of(me), block_of(me), asem, 7))
+        picked.append(to(cpeer, block_of(me), block_of(me), asem, 8))
+        tick()
+        picked[7].wait_recv()
+        far = (1 - x) * 2 + c
+        picked.append(to(cpeer, block_of(far), block_of(far), asem, 9))
+        picked[8].wait_recv()
+        picked[9].wait_recv()
+        for cp in picked:
+            cp.wait_send()
         for owner in range(8):
-            rows = pl.ds((owner % 4) * 128, 128)
-            part = dg(pick, big[owner // 4, rows, :], 1, 0).astype(bf16)
+            part = big[0, pl.ds(32 * owner, 32), :]
             for block, slot, of, piece in piece_slots():
                 if of == owner:
                     qkv2[pl.ds(block * 32, 32), pl.ds(slot * 128, 128)] = part[:, piece * 128 : piece * 128 + 128]
-        place = placement()
-        joined = dg(qkv2[pl.ds(0, 768), pl.ds(0, 1024)], place, 1, 0).astype(bf16)
+        joined = place(lambda part: qkv2[pl.ds(0, 768), pl.ds(256 * part, 256)]).astype(bf16)
         for block in range(24):
             ad[:, pl.ds(block * D, D)] = joined[block * 32 : block * 32 + 32]
-        for cp in norms:
+        for cp in small[7:]:
             cp.wait_recv()
         for j in range(8):
             qkv2[pl.ds(0, 16), pl.ds(j * 128, 128)] = nbuf[pl.ds(16 * j, 16), :]
-        nm[...] = dg(qkv2[pl.ds(0, 16), pl.ds(0, 1024)], place, 1, 0)
+        nm[...] = place(lambda part: qkv2[pl.ds(0, 16), pl.ds(256 * part, 256)])
     else:
         need("ad")
         need("nm")
     arrive()
     for i in range(4):
         xt.put(dg(onehot(to_patches(i), R), rcv_a[...], 1, 0).astype(bf16), pl.ds(i * GR, GR))
+    tick()
     norm(0, lambda rows: xt.get(rows).astype(f32), lambda rows, v: h1.put(v, rows))
-    need("q0")
-    forward(0, h1, wq.at[0], QKV, 768, mask_t, lambda c, acc: qkv1.put(acc.astype(bf16), off=c), tick)
-    temporal_loop(lambda rows, n, off, bias: attend_pair(qkv1, rows, n, off, bias, o1), tick)
+    tick()
+    forward(0, h1, wq.at[0], QKV, 768, mask_t, lambda c, acc: qkv1.put(acc.astype(bf16), off=c), need_tiles("q0"))
+    tick()
+    temporal_loop(lambda rows, n, bias, pairs: attend(qkv1, rows, n, bias, o1, pairs))
+    tick()
     need("p0")
     forward(1, o1, wp.at[0], D, 384, mask_t, lambda c, acc: m1.put(acc.astype(bf16), off=c))
+    tick()
     need("p1")
     forward(2, m1, wp.at[1], D, 384, mask_t, lambda c, acc: spare.put(acc.astype(bf16), off=c))
     tick()
@@ -562,29 +687,35 @@
         cp.start()
     for cp in saves:
         cp.wait()
+    tick()
 
     need("o")
-    backward(6, p_a1, wo, FF, 768, mask_s, lambda c, acc: p_d.put(acc.astype(bf16), off=c))
-    us[8] = us[7]
+    backward(6, p_a1, wo, FF, 768, mask_s, lambda c, acc: p_d.put(acc.astype(bf16), off=c), lambda c: tick())
+    us[:, pl.ds(256, 32)] = us[:, pl.ds(224, 32)]
+    tick()
     arrive()
+    tick()
 
     for g in range(4):
         rows = pl.ds(g * GR, GR)
         tb = dg(onehot(to_frames(g), R), rcv_b[...], 1, 0)
         x1[rows, :] = a0[rows, :].astype(f32) + tb
+    tick()
     norm(1, lambda rows: x1[rows, :], lambda rows, v: p_o2.put(v, rows))
-    need("q1")
-    forward(3, p_o2, wq.at[1], QKV, 768, mask_s, lambda c, acc: p_qkv2.put(acc.astype(bf16), off=c), tick)
-    spatial_loop(lambda rows, n, off, bias: attend_pair(p_qkv2, rows, n, off, bias, p_o2), tick)
+    tick()
+    forward(3, p_o2, wq.at[1], QKV, 768, mask_s, lambda c, acc: p_qkv2.put(acc.astype(bf16), off=c), need_tiles("q1"))
+    tick()
+    spatial_loop(3, lambda rows, n, bias, pairs: attend(p_qkv2, rows, n, bias, p_o2, pairs))
+    tick()
     need("p2")
 
     def add_spatial(c, acc):
         x2[:, cols(c, 384)] = x1[:, cols(c, 384)] + acc
 
     forward(4, p_o2, wp.at[2], D, 384, mask_s, add_spatial)
+    tick()
 
     norm(2, lambda rows: x2[rows, :], lambda rows, v: p_a0.put(v, rows))
-    need("i")
 
     def activate(c, acc):
         tmp_w = acc.shape[1]
@@ -598,7 +729,7 @@
             p_g.put((v * phi).astype(bf16), rows, c)
             p_d.put((p_d.get(rows, c, tmp_w).astype(f32) * slope).astype(bf16), rows, c)
 
-    forward(5, p_a0, wi, FF, 768, mask_s, activate)
+    forward(5, p_a0, wi, FF, 768, mask_s, activate, need_tiles("i"))
 
     def emit_out(c, acc):
         y = (x2[:, cols(c, 384)] + acc).astype(bf16)
@@ -606,12 +737,12 @@
             out[g // 2, g % 2, :, cols(c, 384)] = y[g * GR : g * GR + NP]
 
     forward(6, p_g, wo, D, 384, mask_s, emit_out)
-    us[7] = us[8]
+    us[:, pl.ds(224, 32)] = us[:, pl.ds(256, 32)]
     adapter_grads(6, p_g, p_a1)
 
     if gathers:
         net.finish()
-        for cp in norms:
+        for cp in small:
             cp.wait_send()
 
     def emit_tmp(c, acc):
@@ -632,7 +763,7 @@
 
     backward(4, p_a0, wp.at[2], D, 384, mask_s, lambda c, acc: p_a1.put(acc.astype(bf16), off=c))
     adapter_grads(4, p_o2, p_a0)
-    spatial_loop(lambda rows, n, off, bias: attend_pair_back(p_qkv2, rows, n, off, bias, p_a1))
+    spatial_loop(2, lambda rows, n, bias, pairs: attend_back(p_qkv2, rows, n, bias, p_a1, pairs, False))
     backward(3, p_qkv2, wq.at[1], D, 384, mask_s, emit_tmp)
 
     def step_one(rows):
@@ -648,30 +779,54 @@
         cp.wait()
     arrive()
 
+    if gathers:
+        first, second = (Reduce(i, gd, wi, wo, received, grads, nidx, bsem) for i in range(2))
+        first.split()
     for i in range(4):
         p_a0.put(dg(onehot(to_patches(i), R), rcv_a[...], 1, 0).astype(bf16), pl.ds(i * GR, GR))
     backward(2, p_a0, wp.at[1], D, 384, mask_t, lambda c, acc: p_a1.put(acc.astype(bf16), off=c))
     adapter_grads(2, m1, p_a0)
+    if gathers:
+        first.over_x()
     backward(1, p_a1, wp.at[0], D, 384, mask_t, lambda c, acc: spare.put(acc.astype(bf16), off=c))
     adapter_grads(1, o1, p_a1)
-    temporal_loop(lambda rows, n, off, bias: attend_pair_back(qkv1, rows, n, off, bias, spare))
-    backward(0, qkv1, wq.at[0], D, 384, mask_t, emit_tmp)
+    temporal_loop(lambda rows, n, bias, pairs: (attend_back(qkv1, rows, n, bias, spare, pairs[:3], True), attend_back(qkv1, rows, n, bias, spare, pairs[3:], True)))
+    if gathers:
+        first.to_owners()
+    rank_back(0, qkv1, mask_t)
+    adapter_grads(0, h1, qkv1)
+    if gathers:
+        second.split()
+        first.by_adapter()
+    backward_rows(0, qkv1, wq.at[0], D, 384, emit_tmp)
+    if gathers:
+        second.over_x()
+        first.spread()
 
     def step_zero(rows):
         dx = norm_back_rows(xt.get(rows).astype(f32), gain(0), tmp[rows, :])
         a0[rows, :] = dx.astype(bf16)
 
     chunks(64, step_zero)
+    if gathers:
+        second.to_owners()
     arrive = exchange(3, p_a0, from_patches, rcv_b)
-    adapter_grads(0, h1, qkv1)
+    if gathers:
+        second.by_adapter()
+        first.finish()
+        second.spread()
     arrive()
     for g in range(4):
         dxt = dg(onehot(to_frames(g), R), rcv_b[...], 1, 0)
         total = x2[pl.ds(g * GR, GR), :] + dxt
         ig[g // 2, g % 2] = total.astype(bf16)[:NP]
-
-
-def layer(gathers, idx, x, g, hq, hp, hi, ho, ad, nm):
+    if gathers:
+        second.finish()
+    else:
+        grads[...] = gd[...]
+
+
+def layer(gathers, index_rows, x, g, hq, hp, hi, ho, ad, nm):
     vm = pl.BlockSpec(memory_space=pltpu.VMEM)
     hbm = pl.BlockSpec(memory_space=pl.ANY)
     dma = pltpu.SemaphoreType.DMA
@@ -682,23 +837,24 @@
         out_shape=[
             jax.ShapeDtypeStruct(x.shape, bf16),
             jax.ShapeDtypeStruct(x.shape, bf16),
-            jax.ShapeDtypeStruct((32, ADW), bf16),
+            jax.ShapeDtypeStruct((128, 24 * 128) if gathers else (32, ADW), bf16),
             jax.ShapeDtypeStruct((2, R, FF), bf16),
         ],
-        in_specs=[pl.BlockSpec(memory_space=pltpu.SMEM)] + [hbm] * 8,
+        in_specs=[hbm] * 9,
         out_specs=[vm] * 3 + [hbm],
         scratch_shapes=[
             pltpu.VMEM((2, D, QKV), bf16), pltpu.VMEM((3, D, D), bf16), pltpu.VMEM((D, FF), bf16), pltpu.VMEM((FF, D), bf16),
             pltpu.VMEM((32, ADW), bf16), pltpu.VMEM((16, D), f32), pltpu.VMEM((128, 128), bf16),
-            pltpu.VMEM((3 * GR, D), bf16), rows(D), rows(D), pltpu.VMEM((2, R, FF), bf16), rows(D, f32), rows(D, f32), rows(D, f32),
-            rows(D), rows(QKV), rows(D), rows(D), pltpu.VMEM((9, R, 32), bf16),
-            dma((11,)), dma((4, 3)), dma((4, 3)), dma((2,)), dma((22 * ng,)), dma((22 * ng,)), dma((2, 7)),
+            pltpu.VMEM((256, 128), jnp.int32), pltpu.VMEM((32, ADW), bf16), pltpu.VMEM((256, D), bf16),
+            rows(D), rows(D), pltpu.VMEM((2, R, FF), bf16), rows(D, f32), rows(D, f32), rows(D, f32),
+            rows(D), rows(QKV), rows(D), rows(D), rows(384),
+            dma((12,)), dma((4, 3)), dma((4, 3)), dma((2,)), dma((22 * ng,)), dma((22 * ng,)), dma((2, 14)), dma((2, 10)), dma((2, 32)),
         ],
         compiler_params=pltpu.CompilerParams(
             collective_id=1, has_side_effects=True, vmem_limit_bytes=64 * 2**20 - 2**17
         ),
         name="layer",
-    )(idx, x, g, hq, hp, hi, ho, ad, nm)
+    )(index_rows, x, g, hq, hp, hi, ho, ad, nm)
 
 
 def piece_widths(w):
@@ -764,12 +920,16 @@
     packed = pack_adapters(adapt_down, adapt_down_wide, adapt_up_qkv, adapt_up, adapt_up_wide)
     norms = jnp.concatenate([norm_gain, norm_bias], axis=0)
     if owners == 8:
+        index_rows = adapter_index[:, None] * RANK + jnp.arange(RANK, dtype=jnp.int32)[None, :]
+        index_rows = jnp.broadcast_to(index_rows.reshape(clips * RANK, 1), (clips * RANK, 128))
         pieces = packed.reshape(adapters * RANK, 24, w)
         table = jnp.pad(pieces, ((0, 0), (0, 0), (0, 128 - w))).reshape(adapters * RANK, 24 * 128)
         own_norms = jnp.pad(norms, ((0, 10), (0, 128 - w)))
         output, input_grad, grads, _ = layer(
-            True, adapter_index, inputs, out_grad, qkv_weight, proj_weight, mlp_in, mlp_out, table, own_norms
+            True, index_rows, inputs, out_grad, qkv_weight, proj_weight, mlp_in, mlp_out, table, own_norms
         )
+        grads = grads.reshape(adapters, RANK, 24, 128)[..., :w].astype(f32)
+        summed = jnp.concatenate([grads[:, :, PLACES[p]] for p in range(24)], axis=-1)
     else:
         full_qkv = lax.all_gather(qkv_weight, "clip", axis=1, tiled=True)
         full_proj = lax.all_gather(proj_weight, "clip", axis=1, tiled=True)
@@ -783,14 +943,14 @@
         output, input_grad, grads, _ = layer(
             False, adapter_index, inputs, out_grad, full_qkv, full_proj, full_in, full_out, ad, nm
         )
-    parts = split_pieces(grads, w, owners)
-    parts = lax.all_to_all(parts, "clip", split_axis=0, concat_axis=0, tiled=True)
-    every = lax.all_gather(adapter_index, "clip", axis=0, tiled=True)
-    pick = (every[:, None] == jnp.arange(adapters, dtype=jnp.int32)[None, :]).astype(bf16)
-    summed = jnp.einsum(
-        "ca,crm->arm", pick, parts.reshape(owners * clips, RANK, 24 * w), preferred_element_type=f32
-    )
-    summed = lax.psum(summed.astype(bf16), "frame").astype(f32)
+        parts = split_pieces(grads, w, owners)
+        parts = lax.all_to_all(parts, "clip", split_axis=0, concat_axis=0, tiled=True)
+        every = lax.all_gather(adapter_index, "clip", axis=0, tiled=True)
+        pick = (every[:, None] == jnp.arange(adapters, dtype=jnp.int32)[None, :]).astype(bf16)
+        summed = jnp.einsum(
+            "ca,crm->arm", pick, parts.reshape(owners * clips, RANK, 24 * w), preferred_element_type=f32
+        )
+        summed = lax.psum(summed.astype(bf16), "frame").astype(f32)
     return (output, input_grad) + unpack_grads(summed, w)
 
 

time: 459 us -> 340 us (0.74)
  blocking collectives: 29.2 us -> 0 us
  waiting for transfers between devices: 27.9 us -> 0 us
  Pallas kernels: 339 us -> 312 us
  between operations: 15.6 us -> 1.04 us
  local copies, waits for them, and re-layouts: 28.4 us -> 15.8 us
  starting transfers between devices: 9.02 us -> 0 us
    unnamed x1 -> x0, blocking collectives: 29.2 us -> none
    psum x1 -> x0, waiting for transfers between devices: 27.9 us -> none  [per_device(): summed = lax.psum(summed.astype(bf16), 'frame').astype(f32)]
    pallas_call x1, Pallas kernels: 339 us -> 312 us  [layer(): pl.pallas_call(functools.partial(layer_kernel, gathers), out_shape=[jax.S...]
    all_to_all x1 -> x0, starting transfers between devices: 8.99 us -> none  [per_device(): lax.all_to_all(parts, 'clip', split_axis=0, concat_axis=0, tiled=True)]
    unnamed x35 -> x20, local copies, waits for them, and re-layouts: 11.5 us -> 9.24 us
  transfers between devices with their start and end apart: 2 -> 0, of which waited for: 1 -> 0; matrix products, arithmetic and copies ran while one was open for 1% -> 0% of each run, Pallas kernels for 0% -> 0%
where the time goes in v3:
time: 340 us; the launch traced here: 333 us
  Pallas kernels  312 us (92%)
  local copies, waits for them, and re-layouts  15.8 us (5%)
  other arithmetic  4.75 us (1%)
    pallas_call x1, Pallas kernels, layer(): pl.pallas_call(functools.partial(layer_kernel, gathers), out_shape=[jax.S...  312 us
    unnamed x20, local copies, waits for them, and re-layouts  9.24 us

profile of v3, /device:TPU:0, one launch (start us, length us, event | category | flops | bytes accessed | tf_op | source)
XLA Modules:
  0.0 333.3 jit_solution(6348123506362375524)
XLA Ops:
  0.6 0.0 copy-start.6
  0.6 0.0 copy-start.5
  0.7 0.0 copy-start.4
  0.7 0.7 broadcast_multiply_fusion
  1.4 0.1 iota_add_fusion
  1.5 0.1 add.27
  1.5 1.3 fusion.5.hnm
  2.8 0.7 broadcast_in_dim.2.hidx
  3.5 1.0 copy.29
  4.5 0.1 reshape.76
  4.7 1.1 copy.28
  5.8 0.2 reshape.75
  6.0 0.0 copy-done.4
  6.0 0.1 copy.27
  6.1 0.2 reshape.74
  6.3 0.0 copy-done.6
  6.3 0.0 copy-done.5
  6.3 0.4 concatenate.27
  6.7 1.2 reshape.77
  7.9 0.0 copy-start.1
  7.9 0.2 pad.8
  8.1 1.0 copy.42
  9.1 0.0 copy-start.2
  9.1 0.1 copy-done.1
  9.3 1.1 copy.30.x_ref
  10.4 0.3 copy-done.2
  10.7 1.2 copy.31.g_ref
  11.9 311.6 %layer.1 = (bf16[2,2,196,768]{3,2,1,0:T(8,128)(2,1)}, bf16[2,2,196,768]{3,2,1,0:T(8,128)(2,1)}, bf16[128,3072]{1,0:T(8,128)(2,1)}, bf16[2,832,3072]{2,1,0:T(8,128)(2,1)}) custom-call(s32[32,128]{1,0:T(8,128)} %broadcast_in_dim.2.hidx, bf16[2,2,196,768]{3,2,1,0:T(8,128)(2,1)} %copy.30.x_ref, bf16[2,2,196,768]{3,2,1,0:T(8,128)(2,1)} %copy.31.g_ref, ...), custom_call_target="tpu_custom_call" | custom-call | tf_op jit(solution)/shard_map/layer/pallas_call | solution.py:835
  323.5 0.0 copy-start.3
  323.5 3.3 copy.34
  326.8 0.0 copy-done.3
  326.8 0.2 copy.38
  327.0 0.2 copy_convert_fusion
  327.2 0.7 maximum_bitcast_fusion.1
  327.9 0.1 slice_bitcast_fusion.3
  328.0 1.0 maximum_bitcast_fusion.2
  329.0 0.8 maximum_bitcast_fusion
  329.8 0.0 copy-start
  329.8 0.2 concatenate.31
  330.0 0.3 reshape.80
  330.3 0.8 copy.43
  331.0 0.0 copy-done
  331.1 1.9 copy.35
  (2 shorter events, 0.0 us)
Async XLA Ops:
  0.6 5.7 %copy-start.6 = (bf16[8,16,384]{2,1,0:T(8,128)(2,1)S(1)}, bf16[8,16,384]{2,1,0:T(8,128)(2,1)}, u32[]{:S(2)}) copy-start(bf16[8,16,384]{2,1,0:T(8,128)(2,1)} %param.27) | copy-start | bytes 294916
  0.6 5.7 %copy-start.5 = (bf16[8,384,16]{1,2,0:T(8,128)(2,1)S(1)}, bf16[8,384,16]{1,2,0:T(8,128)(2,1)}, u32[]{:S(2)}) copy-start(bf16[8,384,16]{1,2,0:T(8,128)(2,1)} %param.24) | copy-start | bytes 294916
  0.7 5.3 %copy-start.4 = (bf16[6,8,96,16]{2,3,1,0:T(8,128)(2,1)S(1)}, bf16[6,8,96,16]{2,3,1,0:T(8,128)(2,1)}, u32[]{:S(2)}) copy-start(bf16[6,8,96,16]{2,3,1,0:T(8,128)(2,1)} %param.23) | copy-start | bytes 442372
  7.9 1.3 copy-start.1
  9.1 1.5 copy-start.2
  323.5 3.3 copy-start.3
  329.8 1.3 copy-start
